TPU v7x, 256 devices: a whole 4x4x8 slice. The times are simulated.
256 devices in a mesh: dp: 2 (over core), seq: 32 (over z, y), head: 4 (over x).
Axes of the slice: x: 4, y: 4, z: 8, core: 2. Of those that a mesh axis runs over, the one named last changes fastest.
Arguments:
- prompt_key_input: bfloat16 [2, 6144, 512], P('dp', 'seq', 'head'), may hold values from -6 to 6
- prompt_value_input: bfloat16 [2, 6144, 512], P('dp', 'seq', 'head'), may hold values from -6 to 6
- resp_queries: bfloat16 [2, 32, 128, 4096], P('dp', 'seq', None, 'head'), may hold values from -6 to 6
- response_key_input: bfloat16 [2, 32, 128, 512], P('dp', 'seq', None, 'head'), may hold values from -6 to 6
- response_value_input: bfloat16 [2, 32, 128, 512], P('dp', 'seq', None, 'head'), may hold values from -6 to 6
- q_gain: float32 [128], replicated, may hold values from 0.5 to 3.5
- k_gain: float32 [128], replicated, may hold values from 0.5 to 3.5
- groups: int32 [2, 32], P('dp', 'seq'), may hold values from 0 to 1, as said below
- lengths: int32 [2, 32], P('dp', 'seq'), may hold values from 32 to 128, as said below
- tiles: int32 [2, 32, 48], P('dp', 'seq'), may hold values 0 or 1
- advantages: float32 [2, 32], P('dp', 'seq'), may hold values from -3 to 3
- upstream: bfloat16 [2, 32, 128, 4096], P('dp', 'seq', None, 'head'), may hold values from -6 to 6
Outputs:
- response_query_gradient: float32 [2, 32, 128, 4096], P('dp', 'seq', 'head')
- response_key_gradient: float32 [2, 32, 128, 512], P('dp', 'seq', None, 'head')
- grad_resp_values: float32 [2, 32, 128, 512], P('dp', 'seq', None, 'head')
- prompt_key_gradient: float32 [2, 6144, 512], P('dp', 'seq', 'head')
- prompt_value_gradient: float32 [2, 6144, 512], P('dp', 'seq', 'head')
- query_gain_gradient: float32 [128], replicated
- grad_k_gain: float32 [128], replicated
Inputs may be any that keep to these rules, and one draw needn't show every extreme that they name: `groups`: each prompt 0 to 1 of a set is named by exactly 16 of its responses. `lengths`: in each set some response has length 128.
All inputs are finite; a program needn't handle non-finite values. No bound on the sum of `tiles` on one device may be relied on, other than what follows from the above.
Results may differ from a plain program's by a relative error of at most 0.008.
The roundings to bfloat16 on the way count: a program that leaves them out, or rounds other values in their place, can miss the bound.
Values may be sent and summed in bfloat16 or wider, within the bound.
No kernel may reach another device: no remote copies, remote signals or barrier semaphores. Data moves between devices by JAX's collectives and lax.ppermute only.
A program may use at most 128 MiB of HBM per device.

v0:
```python
import functools

import jax
import jax.numpy as jnp
from jax import lax
from jax.experimental import pallas as pl
from jax.experimental.pallas import tpu as pltpu
from jax.sharding import Mesh
from jax.sharding import PartitionSpec as P

TILE = 64
HEAD = 128
HEADS = 8
TOKENS = 128
QUERIES = HEADS * TOKENS
ROWS = 192
Z = 8
Y = 4
X = 4
QUARTER = ROWS * Z // 2
BLOCK = 256
PART = TOKENS // X
PER_ROWS = ROWS // TILE
PER_PROMPT = PER_ROWS * Y
EPSILON = 1e-06
NEGATIVE = -1e30
SCALE = HEAD ** (-0.5)
SCALE2 = SCALE * 1.4426950408889634
VMEM = 56 * 1024 * 1024
SMALL = 12 * 1024 * 1024
F32 = jnp.float32
BF16 = jnp.bfloat16


def dot_nt(a, b):
    return lax.dot_general(a, b, (((1,), (1,)), ((), ())), preferred_element_type=F32)


def dot_nn(a, b):
    return jnp.dot(a, b, preferred_element_type=F32)


def dot_tn(a, b):
    return lax.dot_general(a, b, (((0,), (0,)), ((), ())), preferred_element_type=F32)


def unit(x):
    return x * lax.rsqrt(jnp.mean(x * x, axis=-1, keepdims=True) + EPSILON)


def norm_back(x, g, dy):
    r = lax.rsqrt(jnp.mean(x * x, axis=-1, keepdims=True) + EPSILON)
    u = x * r
    gy = g * dy
    return r * (gy - u * jnp.mean(u * gy, axis=-1, keepdims=True))


def responder(y, k):
    return lax.rem(y + (0, 1, 3, 2)[k], Y)


def heads_of(ref, first, count):
    return jnp.concatenate(
        [ref[:, j * HEAD : (j + 1) * HEAD] for j in range(first, first + count)], axis=0
    )


def tile_bias(info, who, y, t):
    index = 1 + (t // PER_ROWS) * PER_PROMPT + y * PER_ROWS + t % PER_ROWS
    return jnp.where(info[who, index] > 0, 0.0, NEGATIVE).astype(F32)


def causal():
    v = lax.broadcasted_iota(jnp.int32, (TOKENS, QUERIES), 0)
    t = lax.broadcasted_iota(jnp.int32, (TOKENS, QUERIES), 1) % TOKENS
    return v <= t


def joined(ref, k, first, count):
    return jnp.concatenate([ref[k, h : h + 1, :] for h in range(first, first + count)], axis=1)


def tiles_of(x):
    return [x[t * TILE : (t + 1) * TILE] for t in range(QUARTER // TILE)]


def biases_of(info, who, y):
    return [tile_bias(info, who, y, t) for t in range(QUARTER // TILE)]


def terms_of(rest):
    terms = []
    for _ in range(3):
        terms.append(rest.astype(BF16))
        rest = rest - terms[-1].astype(F32)
    return terms


def stats_kernel(pos, info, qg, kg, *refs):
    q = refs[:4]
    kv = refs[4]
    kr = refs[5]
    qh, kh, krh, out = refs[6:]
    y = pos[0]
    kh[...] = (unit(kv[:, :HEAD].astype(F32)) * kg[...]).astype(BF16)
    krh[...] = (unit(kr[...].astype(F32)) * kg[...]).astype(BF16)
    for k in range(4):
        for j in range(HEADS):
            u = unit(q[k][:TOKENS, j * HEAD : (j + 1) * HEAD].astype(F32))
            qh[k, j * TOKENS : (j + 1) * TOKENS, :] = (u * qg[...]).astype(BF16)
    own = jnp.where(causal(), dot_nt(krh[...], qh[0]) * SCALE2, NEGATIVE)
    own_top = jnp.max(own, axis=0, keepdims=True)
    own_sum = jnp.sum(jnp.exp2(own - own_top), axis=0, keepdims=True)
    for k in range(4):
        who = responder(y, k)
        first = pl.multiple_of(info[k, 0] * QUARTER, QUARTER)
        keys = kh[pl.ds(first, QUARTER), :]
        bias = biases_of(info, k, y)
        for b in range(QUERIES // BLOCK):
            qb = qh[k, b * BLOCK : (b + 1) * BLOCK, :]
            tiles = tiles_of(dot_nt(keys, qb) * SCALE2)
            top = functools.reduce(
                jnp.maximum,
                [jnp.max(a, axis=0, keepdims=True) + v for a, v in zip(tiles, bias)],
            )
            top = jnp.maximum(top, 0.1 * NEGATIVE)
            total = sum(
                jnp.sum(jnp.exp2(a - (top - v)), axis=0, keepdims=True) for a, v in zip(tiles, bias)
            )
            if k == 0:
                span = slice(b * BLOCK, (b + 1) * BLOCK)
                both = jnp.maximum(top, own_top[:, span])
                total = total * jnp.exp2(top - both) + own_sum[:, span] * jnp.exp2(
                    own_top[:, span] - both
                )
                top = both
            for h in range(BLOCK // TOKENS):
                row = b * (BLOCK // TOKENS) + h
                span = slice(h * TOKENS, (h + 1) * TOKENS)
                out[who, row : row + 1, :] = top[:, span]
                out[who, 8 + row : 9 + row, :] = total[:, span]


def values_kernel(pos, info, qh, kh, kv, krh, vr, *refs):
    st = refs[:4]
    go = refs[4:8]
    dv_out, dvr, lt, out, dv = refs[8:]
    y = pos[0]
    for k in range(4):
        who = responder(y, k)
        top = functools.reduce(jnp.maximum, [s[who, 0:8, :] for s in st])
        total = sum(s[who, 8:16, :] * jnp.exp2(s[who, 0:8, :] - top) for s in st)
        lt[k, :, :] = top + jnp.log2(total)
    dv[...] = jnp.zeros_like(dv)
    gb = heads_of(go[0], 0, HEADS)
    s = dot_nt(krh[...], qh[0]) * SCALE2
    p = jnp.where(causal(), jnp.exp2(s - joined(lt, 0, 0, HEADS)), 0.0).astype(BF16)
    own_dots = jnp.sum(p.astype(F32) * dot_nt(vr[...], gb), axis=0, keepdims=True)
    dvr[...] = dot_nn(p, gb)
    for k in range(4):
        who = responder(y, k)
        rows = pl.ds(pl.multiple_of(info[k, 0] * QUARTER, QUARTER), QUARTER)
        bias = biases_of(info, k, y)
        for b in range(QUERIES // BLOCK):
            per = BLOCK // TOKENS
            qb = qh[k, b * BLOCK : (b + 1) * BLOCK, :]
            gb = heads_of(go[k], b * per, per)
            row = joined(lt, k, b * per, per)
            scores = tiles_of(dot_nt(kh[rows, :], qb) * SCALE2)
            grads = tiles_of(dot_nt(kv[rows, HEAD:], gb))
            dots = own_dots[:, b * BLOCK : (b + 1) * BLOCK] if k == 0 else 0.0
            parts = []
            for a, g, v in zip(scores, grads, bias):
                p = jnp.exp2(a - (row - v)).astype(BF16)
                parts.append(p)
                dots = dots + jnp.sum(p.astype(F32) * g, axis=0, keepdims=True)
            dv[rows, :] += dot_nn(jnp.concatenate(parts, axis=0), gb)
            for h in range(per):
                out[who, b * per + h : b * per + h + 1, :] = dots[:, h * TOKENS : (h + 1) * TOKENS]
    dv_out[...] = dv[...].astype(BF16)


def grads_kernel(pos, info, lt, qh, kh, kv, krh, vr, kg, kr, dv, *refs):
    dd = refs[:4]
    go = refs[4:8]
    q = refs[8:12]
    dq = refs[12:15]
    far, out, dkr, kt, dk = refs[15:]
    y = pos[0]
    for p in range(2):
        kt[p, :, :] = kh[p * QUARTER : (p + 1) * QUARTER, :].T
    dk[...] = jnp.zeros_like(dk)
    gb = heads_of(go[0], 0, HEADS)
    dot_rows = []
    for k in range(4):
        who = responder(y, k)
        dots = sum(d[who] for d in dd)
        dot_rows.append(dots)
    s = dot_nt(krh[...], qh[0]) * SCALE2
    p = jnp.where(causal(), jnp.exp2(s - joined(lt, 0, 0, HEADS)), 0.0)
    every = jnp.concatenate([dot_rows[0][h : h + 1] for h in range(HEADS)], axis=1)
    ds = (p * (dot_nt(vr[...], gb) - every)).astype(BF16)
    own = dot_nn(ds, qh[0]) * SCALE
    own_dq = dot_nn(krh[...].T, ds)
    x = kr[...].astype(F32)
    dkr[...] = norm_back(x, kg[...], own)
    gain_k = jnp.sum(own * unit(x), axis=0, keepdims=True)
    gain_q = jnp.zeros((1, HEAD), F32)
    for k in (3, 1, 2, 0):
        who = responder(y, k)
        group = info[k, 0]
        rows = pl.ds(pl.multiple_of(group * QUARTER, QUARTER), QUARTER)
        bias = biases_of(info, k, y)
        for b in range(QUERIES // BLOCK):
            per = BLOCK // TOKENS
            qb = qh[k, b * BLOCK : (b + 1) * BLOCK, :]
            gb = heads_of(go[k], b * per, per)
            row = joined(lt, k, b * per, per)
            dots = jnp.concatenate(
                [dot_rows[k][b * per + h : b * per + h + 1] for h in range(per)], axis=1
            )
            scores = tiles_of(dot_nt(kh[rows, :], qb) * SCALE2)
            grads = tiles_of(dot_nt(kv[rows, HEAD:], gb))
            ds = jnp.concatenate(
                [
                    (jnp.exp2(a - (row - v)) * (g - dots)).astype(BF16)
                    for a, g, v in zip(scores, grads, bias)
                ],
                axis=0,
            )
            dk[rows, :] += dot_nn(ds, qb)
            total = dot_nn(kt[group], ds)
            if k == 0:
                total = total + own_dq[:, b * BLOCK : (b + 1) * BLOCK]
            total = total * SCALE
            for h in range(per):
                j = b * per + h
                part = total[:, h * TOKENS : (h + 1) * TOKENS].T
                if k == 3:
                    lane = j % (HEADS // 2) * HEAD
                    far[j // (HEADS // 2), :, lane : lane + HEAD] = part
                else:
                    dq[k][:, j * HEAD : (j + 1) * HEAD] = part
                u = unit(q[k][:TOKENS, j * HEAD : (j + 1) * HEAD].astype(F32))
                gain_q = gain_q + jnp.sum(part * u, axis=0, keepdims=True)
    scaled = dk[...] * SCALE
    for c in range(Z):
        span = slice(c * ROWS, (c + 1) * ROWS)
        out[c, :ROWS, :HEAD] = scaled[span].astype(BF16)
        out[c, :ROWS, HEAD:] = dv[span, :]
    u = unit(kv[:, :HEAD].astype(F32))
    gain_k = gain_k + jnp.sum(scaled * u, axis=0, keepdims=True)
    terms = terms_of(jnp.concatenate([gain_q, gain_k, jnp.zeros((6, HEAD), F32)], axis=0))
    rows = jnp.concatenate([*terms, jnp.zeros((8, HEAD), BF16)], axis=0)
    rows = jnp.concatenate([rows, jnp.zeros_like(rows)], axis=1)
    for c in range(Z):
        out[c, ROWS:, :] = rows


def query_back_kernel(q, qg, mine, left, right, gains, out):
    for j in range(HEADS):
        span = slice(j * HEAD, (j + 1) * HEAD)
        dy = mine[:, span] + left[:, span] + right[:, span]
        dx = norm_back(q[:, span].astype(F32), qg[...], dy).astype(BF16)
        for h in range(X):
            out[h, :PART, span] = dx[h * PART : (h + 1) * PART]
    terms = terms_of(sum(gains[i] for i in range(2 * Y)))
    terms.append(jnp.zeros((8, QUERIES - 3 * HEAD), BF16))
    row = jnp.concatenate(terms, axis=1)
    row = jnp.concatenate([row, jnp.zeros_like(row)], axis=0)
    for h in range(X):
        out[h, PART:, :] = row


def key_back_kernel(k, kg, parts, dk, dv):
    total = sum(parts[s, :ROWS, :].astype(F32) for s in range(Z))
    dk[...] = norm_back(k[...].astype(F32), kg[...], total[:, :HEAD])
    dv[...] = total[:, HEAD:]


def spread_kernel(parts, out, gains):
    total = jnp.zeros((8, HEAD), F32)
    for h in range(X):
        out[:, h * QUERIES : (h + 1) * QUERIES] = parts[h, :PART, :].astype(F32)
        rows = parts[h, PART:, :].astype(F32)[0:8]
        total = total + sum(rows[:, i * HEAD : (i + 1) * HEAD] for i in range(3))
    gains[...] = total


def call(kernel, out_shape, n_scalar, args, scratch=(), flops=0, nbytes=0, vmem=SMALL):
    specs = [pl.BlockSpec(memory_space=pltpu.SMEM)] * n_scalar
    specs += [pl.BlockSpec(memory_space=pltpu.VMEM)] * (len(args) - n_scalar)
    return pl.pallas_call(
        kernel,
        out_shape=out_shape,
        in_specs=specs,
        out_specs=jax.tree.map(lambda _: pl.BlockSpec(memory_space=pltpu.VMEM), out_shape),
        scratch_shapes=scratch,
        compiler_params=pltpu.CompilerParams(vmem_limit_bytes=vmem),
        cost_estimate=pl.CostEstimate(flops=flops, bytes_accessed=nbytes, transcendentals=0),
    )(*args)


def f32(*shape):
    return jax.ShapeDtypeStruct(shape, F32)


def bf16(*shape):
    return jax.ShapeDtypeStruct(shape, BF16)


def shift(x, axis, size, step):
    return lax.ppermute(x, axis, [(i, (i + step) % size) for i in range(size)])


def to_all(x, axis):
    return lax.all_to_all(x, axis, 0, 0, tiled=False)


def shards(
    prompt_key_input,
    prompt_value_input,
    resp_queries,
    response_key_input,
    response_value_input,
    q_gain,
    k_gain,
    groups,
    lengths,
    tiles,
    advantages,
    upstream,
):
    y = lax.axis_index("y")
    z = lax.axis_index("z")
    pos = jnp.stack([y, z]).astype(jnp.int32)
    qg = q_gain[None]
    kg = k_gain[None]
    k_raw = prompt_key_input[0]
    q_raw = resp_queries[0, 0]
    kr = response_key_input[0, 0]
    vr = response_value_input[0, 0]
    info = jnp.concatenate([groups[0], tiles[0, 0]]).astype(BF16)
    info = jnp.pad(info[None], ((0, 15), (0, QUERIES - 49)))
    q_ext = jnp.concatenate([q_raw, info], axis=0)

    q_before = shift(q_ext, "y", Y, 1)
    q_next = shift(q_ext, "y", Y, -1)
    q_far = shift(q_before, "y", Y, 1)
    tokens = jnp.arange(TOKENS, dtype=jnp.int32)[:, None]
    go = jnp.where(
        tokens < lengths[0, 0], -advantages[0, 0] * upstream[0, 0].astype(F32), 0.0
    ).astype(BF16)
    go_before = shift(go, "y", Y, 1)
    go_next = shift(go, "y", Y, -1)
    kv = jnp.concatenate([k_raw, prompt_value_input[0]], axis=1)
    kv = to_all(jnp.broadcast_to(kv[None], (Z, ROWS, 2 * HEAD)), "z").reshape(Z * ROWS, 2 * HEAD)
    kv, q_before, q_next, q_far = lax.optimization_barrier((kv, q_before, q_next, q_far))
    go_far = shift(go_next, "y", Y, -1)
    qs = (q_ext, q_next, q_before, q_far)
    gos = (go, go_next, go_before, go_far)
    info = jnp.stack([a[TOKENS, :128] for a in qs]).astype(jnp.int32)

    unit_flops = 2 * 4 * QUERIES * QUARTER * HEAD
    qh, kh, krh, st = call(
        stats_kernel,
        (
            bf16(4, QUERIES, HEAD),
            bf16(2 * QUARTER, HEAD),
            bf16(TOKENS, HEAD),
            f32(Y, 16, 128),
        ),
        2,
        (pos, info, qg, kg, *qs, kv, kr),
        flops=2 * unit_flops,
        nbytes=1 << 22,
        vmem=VMEM,
    )
    sts = [st] + [shift(st, "y", Y, k) for k in (1, -1, 2)]
    dv, dvr, lt, dd = call(
        values_kernel,
        (
            bf16(2 * QUARTER, HEAD),
            f32(TOKENS, HEAD),
            f32(4, HEADS, 128),
            f32(Y, HEADS, 128),
        ),
        2,
        (pos, info, qh, kh, kv, krh, vr, *sts, *gos),
        scratch=[pltpu.VMEM((2 * QUARTER, HEAD), F32)],
        flops=4 * unit_flops,
        nbytes=1 << 22,
        vmem=VMEM,
    )
    dds = [dd] + [shift(dd, "y", Y, k) for k in (1, -1, 2)]
    dq0, dq1, dq2, far, dkv, dkr = call(
        grads_kernel,
        (
            *[f32(TOKENS, QUERIES)] * 3,
            f32(2, TOKENS, QUERIES // 2),
            bf16(Z, ROWS + 32, 2 * HEAD),
            f32(TOKENS, HEAD),
        ),
        2,
        (pos, info, lt, qh, kh, kv, krh, vr, kg, kr, dv, *dds, *gos, *qs),
        scratch=[pltpu.VMEM((2, HEAD, QUARTER), BF16), pltpu.VMEM((2 * QUARTER, HEAD), F32)],
        flops=5 * unit_flops,
        nbytes=1 << 22,
        vmem=VMEM,
    )

    half = QUERIES // 2
    dkvs = to_all(dkv, "z")
    far_up = shift(far[0], "y", Y, 1)
    far_down = shift(far[1], "y", Y, -1)
    to_next = jnp.concatenate([dq1[:, :half] + far_up, dq1[:, half:]], axis=1)
    to_before = jnp.concatenate([dq2[:, :half], dq2[:, half:] + far_down], axis=1)
    from_before = shift(to_next, "y", Y, 1)
    from_next = shift(to_before, "y", Y, -1)
    gains = dkvs[:, ROWS : ROWS + 24, :HEAD].astype(F32).reshape(Z * 3, 8, HEAD).sum(axis=0)
    gains = to_all(jnp.broadcast_to(gains[None], (2 * Y, 8, HEAD)), ("dp", "y"))

    dq = call(
        query_back_kernel,
        bf16(X, PART + 16, QUERIES),
        0,
        (q_raw, qg, dq0, from_before, from_next, gains),
        nbytes=1 << 21,
    )
    dq = to_all(dq, "head")
    regrouped, gains = call(
        spread_kernel, (f32(PART, X * QUERIES), f32(8, HEAD)), 0, (dq,), nbytes=1 << 20
    )
    dk, dv = call(
        key_back_kernel,
        (f32(ROWS, HEAD), f32(ROWS, HEAD)),
        0,
        (k_raw, kg, dkvs),
        nbytes=1 << 20,
    )
    return (
        regrouped[None, None],
        dkr[None, None],
        dvr[None, None],
        dk[None],
        dv[None],
        gains[0],
        gains[1],
    )


def solution(mesh):
    sizes = mesh.devices.shape
    split = Mesh(mesh.devices.reshape(sizes[0], Z, Y, sizes[2]), ("dp", "z", "y", "head"))
    seq = ("z", "y")
    placed = (
        P("dp", seq, "head"),
        P("dp", seq, "head"),
        P("dp", seq, None, "head"),
        P("dp", seq, None, "head"),
        P("dp", seq, None, "head"),
        P(),
        P(),
        P("dp", seq),
        P("dp", seq),
        P("dp", seq, None),
        P("dp", seq),
        P("dp", seq, None, "head"),
    )
    return jax.shard_map(
        shards,
        mesh=split,
        in_specs=placed,
        out_specs=(
            P("dp", seq, "head", None),
            P("dp", seq, None, "head"),
            P("dp", seq, None, "head"),
            P("dp", seq, "head"),
            P("dp", seq, "head"),
            P(),
            P(),
        ),
        check_vma=False,
    )
```

profile of v0, /device:TPU:6, one launch (start us, length us, event | category | flops | bytes accessed | tf_op | source)
XLA Modules:
  0.0 130.2 jit_solution(16329735744088688994)
XLA Ops:
  2.4 8.6 %all-to-all-start = ((bf16[8,192,256]{2,1,0:T(8,128)(2,1)}), bf16[8,192,256]{2,1,0:T(8,128)(2,1)S(1)}, u32[]{:S(2)}, u32[]{:S(2)}) async-start(bf16[8,192,256]{2,1,0:T(8,128)(2,1)} %broadcast_in_dim.48), calls=%async_computation | async-start | bytes 1572864 | tf_op jit(solution)/shard_map/all_to_all | solution.py:317
  14.1 1.7 %collective-permute-start.1 = (bf16[144,1024]{1,0:T(8,128)(2,1)S(1)}, bf16[144,1024]{1,0:T(8,128)(2,1)S(1)}, u32[]{:S(2)}, u32[]{:S(2)}) collective-permute-start(bf16[144,1024]{1,0:T(8,128)(2,1)S(1)} %pad_maximum_fusion.2.refs_0_.refs_8_), channel_id=1, source_target_pairs={{0,12},{4,0},{8,4},{12,8},{1,13},{5,1},{9,5},{13,9},{2,14},{6,2},{... | collective-permute-start | bytes 884744 | tf_op jit(solution)/shard_map/ppermute | solution.py:313
  17.1 5.2 %collective-permute-done.refs_2_.refs_10_ = bf16[144,1024]{1,0:T(8,128)(2,1)S(1)} collective-permute-done((bf16[144,1024]{1,0:T(8,128)(2,1)S(1)}, bf16[144,1024]{1,0:T(8,128)(2,1)S(1)}, u32[]{:S(2)}, u32[]{:S(2)}) %collective-permute-start) | collective-permute-done | bytes 294944 | tf_op jit(solution)/shard_map/ppermute | solution.py:313
  22.7 3.0 %collective-permute-start.6 = (bf16[128,1024]{1,0:T(8,128)(2,1)S(1)}, bf16[128,1024]{1,0:T(8,128)(2,1)S(1)}, u32[]{:S(2)}, u32[]{:S(2)}) collective-permute-start(bf16[128,1024]{1,0:T(8,128)(2,1)S(1)} %fusion.refs_4_), channel_id=1, source_target_pairs={{0,12},{4,0},{8,4},{12,8},{1,13},{5,1},{9,5},{13,9},{2,14},{6,2},{... | collective-permute-start | bytes 786440 | tf_op jit(solution)/shard_map/ppermute | solution.py:313
  26.3 3.5 %collective-permute-done.6.refs_5_ = bf16[128,1024]{1,0:T(8,128)(2,1)S(1)} collective-permute-done((bf16[128,1024]{1,0:T(8,128)(2,1)S(1)}, bf16[128,1024]{1,0:T(8,128)(2,1)S(1)}, u32[]{:S(2)}, u32[]{:S(2)}) %collective-permute-start.6) | collective-permute-done | bytes 262176 | tf_op jit(solution)/shard_map/ppermute | solution.py:313
  29.9 3.7 %collective-permute-start.8 = (bf16[128,1024]{1,0:T(8,128)(2,1)S(1)}, bf16[128,1024]{1,0:T(8,128)(2,1)S(1)}, u32[]{:S(2)}, u32[]{:S(2)}) collective-permute-start(bf16[128,1024]{1,0:T(8,128)(2,1)S(1)} %collective-permute-done.6.refs_5_), channel_id=1, source_target_pairs={{0,12},{4,0},{8,4},{12,8},{1,13},{5,1},{9,5},{13,9},{2,14},{6,2},{... | collective-permute-start | bytes 786440 | tf_op jit(solution)/shard_map/ppermute | solution.py:313
  35.0 7.1 %shard_map.171 = (bf16[4,1024,128]{2,1,0:T(8,128)(2,1)}, bf16[1536,128]{1,0:T(8,128)(2,1)}, bf16[128,128]{1,0:T(8,128)(2,1)}, f32[4,16,128]{2,1,0:T(8,128)}) custom-call(s32[2]{0:T(128)} %pad_add_fusion.pos, s32[4,128]{1,0:T(4,128)} %maximum_convert_fusion.info, f32[1,128]{1,0:T(1,128)} %bitcast.41, f32[1,128]{1,0:T(1,128)} %bitcast.38, ...), custom_call_target="tpu_custom_call" | custom-call | flops 1610612736 | bytes 4194304 | tf_op jit(solution)/shard_map/pallas_call | solution.py:293
  42.1 3.3 %collective-permute-start.5 = (f32[4,16,128]{2,1,0:T(8,128)}, f32[4,16,128]{2,1,0:T(8,128)S(1)}, u32[]{:S(2)}, u32[]{:S(2)}) collective-permute-start(f32[4,16,128]{2,1,0:T(8,128)} %get-tuple-element.36.refs_0_), channel_id=1, source_target_pairs={{0,8},{4,12},{8,0},{12,4},{1,9},{5,13},{9,1},{13,5},{2,10},{6,14},... | collective-permute-start | bytes 98312 | tf_op jit(solution)/shard_map/ppermute | solution.py:313
  47.8 1.7 %collective-permute-done.4.refs_2_ = f32[4,16,128]{2,1,0:T(8,128)S(1)} collective-permute-done((f32[4,16,128]{2,1,0:T(8,128)}, f32[4,16,128]{2,1,0:T(8,128)S(1)}, u32[]{:S(2)}, u32[]{:S(2)}) %collective-permute-start.4) | collective-permute-done | bytes 32800 | tf_op jit(solution)/shard_map/ppermute | solution.py:313
  49.5 2.3 %collective-permute-done.3.refs_1_ = f32[4,16,128]{2,1,0:T(8,128)S(1)} collective-permute-done((f32[4,16,128]{2,1,0:T(8,128)}, f32[4,16,128]{2,1,0:T(8,128)S(1)}, u32[]{:S(2)}, u32[]{:S(2)}) %collective-permute-start.3) | collective-permute-done | bytes 32800 | tf_op jit(solution)/shard_map/ppermute | solution.py:313
  52.4 8.3 %shard_map.172 = (bf16[1536,128]{1,0:T(8,128)(2,1)}, f32[128,128]{1,0:T(8,128)}, f32[4,8,128]{2,1,0:T(8,128)}, f32[4,8,128]{2,1,0:T(8,128)}) custom-call(s32[2]{0:T(128)} %pad_add_fusion.pos, s32[4,128]{1,0:T(4,128)} %maximum_convert_fusion.info, bf16[4,1024,128]{2,1,0:T(8,128)(2,1)} %get-tuple-element.33.qh, bf16[1536,128]{1,0:T(8,128)(2,1)} %get-tuple-element.34.kh, ...), custom_call_target="tpu_custom_call" | custom-call | flops 3221225472 | bytes 4194304 | tf_op jit(solution)/shard_map/pallas_call | solution.py:293
  61.2 2.0 %collective-permute-start.10 = (f32[4,8,128]{2,1,0:T(8,128)}, f32[4,8,128]{2,1,0:T(8,128)S(1)}, u32[]{:S(2)}, u32[]{:S(2)}) collective-permute-start(f32[4,8,128]{2,1,0:T(8,128)} %get-tuple-element.39.refs_0_), channel_id=1, source_target_pairs={{0,12},{4,0},{8,4},{12,8},{1,13},{5,1},{9,5},{13,9},{2,14},{6,2},{... | collective-permute-start | bytes 49160 | tf_op jit(solution)/shard_map/ppermute | solution.py:313
  63.3 2.9 %collective-permute-done.11.refs_3_ = f32[4,8,128]{2,1,0:T(8,128)S(1)} collective-permute-done((f32[4,8,128]{2,1,0:T(8,128)}, f32[4,8,128]{2,1,0:T(8,128)S(1)}, u32[]{:S(2)}, u32[]{:S(2)}) %collective-permute-start.11) | collective-permute-done | bytes 16416 | tf_op jit(solution)/shard_map/ppermute | solution.py:313
  66.2 2.1 %collective-permute-done.9.refs_1_ = f32[4,8,128]{2,1,0:T(8,128)S(1)} collective-permute-done((f32[4,8,128]{2,1,0:T(8,128)}, f32[4,8,128]{2,1,0:T(8,128)S(1)}, u32[]{:S(2)}, u32[]{:S(2)}) %collective-permute-start.9) | collective-permute-done | bytes 16416 | tf_op jit(solution)/shard_map/ppermute | solution.py:313
  69.0 11.2 %shard_map.173 = (f32[128,1024]{1,0:T(8,128)}, f32[128,1024]{1,0:T(8,128)}, f32[128,1024]{1,0:T(8,128)}, f32[2,128,512]{2,1,0:T(8,128)}, bf16[8,224,256]{2,1,0:T(8,128)(2,1)}, /*index=5*/f32[128,128]{1,0:T(8,128)}) custom-call(s32[2]{0:T(128)} %pad_add_fusion.pos, s32[4,128]{1,0:T(4,128)} %maximum_convert_fusion.info, f32[4,8,128]{2,1,0:T(8,128)} %get-tuple-element.37.lt, ...), custom_call_target="tpu_custom_call" | custom-call | flops 4026531840 | bytes 4194304 | tf_op jit(solution)/shard_map/pallas_call | solution.py:293
  80.2 4.0 %all-to-all-start.1 = ((bf16[8,224,256]{2,1,0:T(8,128)(2,1)}), bf16[8,224,256]{2,1,0:T(8,128)(2,1)S(1)}, u32[]{:S(2)}, u32[]{:S(2)}) async-start(bf16[8,224,256]{2,1,0:T(8,128)(2,1)} %get-tuple-element.44), calls=%async_computation.1 | async-start | bytes 1835008 | tf_op jit(solution)/shard_map/all_to_all | solution.py:317
  84.3 3.2 %collective-permute-start.14 = (f32[128,512]{1,0:T(8,128)S(1)}, f32[128,512]{1,0:T(8,128)S(1)}, u32[]{:S(2)}, u32[]{:S(2)}) collective-permute-start(f32[128,512]{1,0:T(8,128)S(1)} %get-tuple-element.53), channel_id=1, source_target_pairs={{0,12},{4,0},{8,4},{12,8},{1,13},{5,1},{9,5},{13,9},{2,14},{6,2},{... | collective-permute-start | bytes 786440 | tf_op jit(solution)/shard_map/ppermute | solution.py:313
  87.5 4.8 %collective-permute-done.12 = f32[128,512]{1,0:T(8,128)S(1)} collective-permute-done((f32[128,512]{1,0:T(8,128)S(1)}, f32[128,512]{1,0:T(8,128)S(1)}, u32[]{:S(2)}, u32[]{:S(2)}) %collective-permute-start.12) | collective-permute-done | bytes 262176 | tf_op jit(solution)/shard_map/ppermute | solution.py:313
  94.4 2.3 %collective-permute-start.15 = (f32[128,1024]{1,0:T(8,128)}, f32[128,1024]{1,0:T(8,128)S(1)}, u32[]{:S(2)}, u32[]{:S(2)}) collective-permute-start(f32[128,1024]{1,0:T(8,128)} %pad_maximum_fusion.1), channel_id=1, source_target_pairs={{0,12},{4,0},{8,4},{12,8},{1,13},{5,1},{9,5},{13,9},{2,14},{6,2},{... | collective-permute-start | bytes 1572872 | tf_op jit(solution)/shard_map/ppermute | solution.py:313
  96.7 10.4 %all-to-all-done.1.parts = bf16[8,224,256]{2,1,0:T(8,128)(2,1)S(1)} async-done(((bf16[8,224,256]{2,1,0:T(8,128)(2,1)}), bf16[8,224,256]{2,1,0:T(8,128)(2,1)S(1)}, u32[]{:S(2)}, u32[]{:S(2)}) %all-to-all-start.1) | async-done | bytes 917536 | tf_op jit(solution)/shard_map/all_to_all | solution.py:317
  107.8 3.3 %all-to-all-start.2 = ((f32[8,8,128]{2,1,0:T(8,128)}), f32[8,8,128]{2,1,0:T(8,128)S(1)}, u32[]{:S(2)}, u32[]{:S(2)}) async-start(f32[8,8,128]{2,1,0:T(8,128)} %broadcast_in_dim.52), calls=%async_computation.2 | async-start | bytes 65536 | tf_op jit(solution)/shard_map/all_to_all | solution.py:317
  111.1 5.2 %all-to-all-done.2.gains = f32[8,8,128]{2,1,0:T(8,128)S(1)} async-done(((f32[8,8,128]{2,1,0:T(8,128)}), f32[8,8,128]{2,1,0:T(8,128)S(1)}, u32[]{:S(2)}, u32[]{:S(2)}) %all-to-all-start.2) | async-done | bytes 32800 | tf_op jit(solution)/shard_map/all_to_all | solution.py:317
  117.7 4.9 %all-to-all-start.3 = ((bf16[4,48,1024]{2,1,0:T(8,128)(2,1)}), bf16[4,48,1024]{2,1,0:T(8,128)(2,1)S(1)}, u32[]{:S(2)}, u32[]{:S(2)}) async-start(bf16[4,48,1024]{2,1,0:T(8,128)(2,1)} %shard_map.174), calls=%async_computation.3 | async-start | bytes 786432 | tf_op jit(solution)/shard_map/all_to_all | solution.py:317
  123.4 5.4 %all-to-all-done.3.parts = bf16[4,48,1024]{2,1,0:T(8,128)(2,1)S(1)} async-done(((bf16[4,48,1024]{2,1,0:T(8,128)(2,1)}), bf16[4,48,1024]{2,1,0:T(8,128)(2,1)S(1)}, u32[]{:S(2)}, u32[]{:S(2)}) %all-to-all-start.3) | async-done | bytes 393248 | tf_op jit(solution)/shard_map/all_to_all | solution.py:317
  (94 shorter events, 17.3 us)
Async XLA Ops:
  2.4 31.7 %all-to-all-start = ((bf16[8,192,256]{2,1,0:T(8,128)(2,1)}), bf16[8,192,256]{2,1,0:T(8,128)(2,1)S(1)}, u32[]{:S(2)}, u32[]{:S(2)}) async-start(bf16[8,192,256]{2,1,0:T(8,128)(2,1)} %broadcast_in_dim.48), calls=%async_computation | async-start | bytes 1572864 | tf_op jit(solution)/shard_map/all_to_all | solution.py:317
  12.4 22.4 %copy-start.9 = (bf16[144,1024]{1,0:T(8,128)(2,1)}, bf16[144,1024]{1,0:T(8,128)(2,1)S(1)}, u32[]{:S(2)}) copy-start(bf16[144,1024]{1,0:T(8,128)(2,1)S(1)} %pad_maximum_fusion.2.refs_0_.refs_8_) | copy-start | bytes 884740
  12.5 9.8 %collective-permute-start = (bf16[144,1024]{1,0:T(8,128)(2,1)S(1)}, bf16[144,1024]{1,0:T(8,128)(2,1)S(1)}, u32[]{:S(2)}, u32[]{:S(2)}) collective-permute-start(bf16[144,1024]{1,0:T(8,128)(2,1)S(1)} %pad_maximum_fusion.2.refs_0_.refs_8_), channel_id=1, source_target_pairs={{0,4},{4,8},{8,12},{12,0},{1,5},{5,9},{9,13},{13,1},{2,6},{6,10},{... | collective-permute-start | bytes 884744 | tf_op jit(solution)/shard_map/ppermute | solution.py:313
  14.1 19.5 %collective-permute-start.1 = (bf16[144,1024]{1,0:T(8,128)(2,1)S(1)}, bf16[144,1024]{1,0:T(8,128)(2,1)S(1)}, u32[]{:S(2)}, u32[]{:S(2)}) collective-permute-start(bf16[144,1024]{1,0:T(8,128)(2,1)S(1)} %pad_maximum_fusion.2.refs_0_.refs_8_), channel_id=1, source_target_pairs={{0,12},{4,0},{8,4},{12,8},{1,13},{5,1},{9,5},{13,9},{2,14},{6,2},{... | collective-permute-start | bytes 884744 | tf_op jit(solution)/shard_map/ppermute | solution.py:313
  22.3 12.5 %copy-start.12 = (bf16[144,1024]{1,0:T(8,128)(2,1)}, bf16[144,1024]{1,0:T(8,128)(2,1)S(1)}, u32[]{:S(2)}) copy-start(bf16[144,1024]{1,0:T(8,128)(2,1)S(1)} %collective-permute-done.refs_2_.refs_10_) | copy-start | bytes 884740
  22.3 11.3 %collective-permute-start.2 = (bf16[144,1024]{1,0:T(8,128)(2,1)S(1)}, bf16[144,1024]{1,0:T(8,128)(2,1)S(1)}, u32[]{:S(2)}, u32[]{:S(2)}) collective-permute-start(bf16[144,1024]{1,0:T(8,128)(2,1)S(1)} %collective-permute-done.refs_2_.refs_10_), channel_id=1, source_target_pairs={{0,4},{4,8},{8,12},{12,0},{1,5},{5,9},{9,13},{13,1},{2,6},{6,10},{... | collective-permute-start | bytes 884744 | tf_op jit(solution)/shard_map/ppermute | solution.py:313
  22.7 19.4 %copy-start.11 = (bf16[128,1024]{1,0:T(8,128)(2,1)}, bf16[128,1024]{1,0:T(8,128)(2,1)S(1)}, u32[]{:S(2)}) copy-start(bf16[128,1024]{1,0:T(8,128)(2,1)S(1)} %fusion.refs_4_) | copy-start | bytes 786436
  22.7 7.2 %collective-permute-start.6 = (bf16[128,1024]{1,0:T(8,128)(2,1)S(1)}, bf16[128,1024]{1,0:T(8,128)(2,1)S(1)}, u32[]{:S(2)}, u32[]{:S(2)}) collective-permute-start(bf16[128,1024]{1,0:T(8,128)(2,1)S(1)} %fusion.refs_4_), channel_id=1, source_target_pairs={{0,12},{4,0},{8,4},{12,8},{1,13},{5,1},{9,5},{13,9},{2,14},{6,2},{... | collective-permute-start | bytes 786440 | tf_op jit(solution)/shard_map/ppermute | solution.py:313
  25.7 21.7 %collective-permute-start.7 = (bf16[128,1024]{1,0:T(8,128)(2,1)S(1)}, bf16[128,1024]{1,0:T(8,128)(2,1)S(1)}, u32[]{:S(2)}, u32[]{:S(2)}) collective-permute-start(bf16[128,1024]{1,0:T(8,128)(2,1)S(1)} %fusion.refs_4_), channel_id=1, source_target_pairs={{0,4},{4,8},{8,12},{12,0},{1,5},{5,9},{9,13},{13,1},{2,6},{6,10},{... | collective-permute-start | bytes 786440 | tf_op jit(solution)/shard_map/ppermute | solution.py:313
  29.9 17.5 %collective-permute-start.8 = (bf16[128,1024]{1,0:T(8,128)(2,1)S(1)}, bf16[128,1024]{1,0:T(8,128)(2,1)S(1)}, u32[]{:S(2)}, u32[]{:S(2)}) collective-permute-start(bf16[128,1024]{1,0:T(8,128)(2,1)S(1)} %collective-permute-done.6.refs_5_), channel_id=1, source_target_pairs={{0,12},{4,0},{8,4},{12,8},{1,13},{5,1},{9,5},{13,9},{2,14},{6,2},{... | collective-permute-start | bytes 786440 | tf_op jit(solution)/shard_map/ppermute | solution.py:313
  42.1 5.7 %collective-permute-start.5 = (f32[4,16,128]{2,1,0:T(8,128)}, f32[4,16,128]{2,1,0:T(8,128)S(1)}, u32[]{:S(2)}, u32[]{:S(2)}) collective-permute-start(f32[4,16,128]{2,1,0:T(8,128)} %get-tuple-element.36.refs_0_), channel_id=1, source_target_pairs={{0,8},{4,12},{8,0},{12,4},{1,9},{5,13},{9,1},{13,5},{2,10},{6,14},... | collective-permute-start | bytes 98312 | tf_op jit(solution)/shard_map/ppermute | solution.py:313
  45.4 4.1 %collective-permute-start.4 = (f32[4,16,128]{2,1,0:T(8,128)}, f32[4,16,128]{2,1,0:T(8,128)S(1)}, u32[]{:S(2)}, u32[]{:S(2)}) collective-permute-start(f32[4,16,128]{2,1,0:T(8,128)} %get-tuple-element.36.refs_0_), channel_id=1, source_target_pairs={{0,12},{4,0},{8,4},{12,8},{1,13},{5,1},{9,5},{13,9},{2,14},{6,2},{... | collective-permute-start | bytes 98312 | tf_op jit(solution)/shard_map/ppermute | solution.py:313
  46.4 5.3 %collective-permute-start.3 = (f32[4,16,128]{2,1,0:T(8,128)}, f32[4,16,128]{2,1,0:T(8,128)S(1)}, u32[]{:S(2)}, u32[]{:S(2)}) collective-permute-start(f32[4,16,128]{2,1,0:T(8,128)} %get-tuple-element.36.refs_0_), channel_id=1, source_target_pairs={{0,4},{4,8},{8,12},{12,0},{1,5},{5,9},{9,13},{13,1},{2,6},{6,10},{... | collective-permute-start | bytes 98312 | tf_op jit(solution)/shard_map/ppermute | solution.py:313
  60.7 5.5 %collective-permute-start.11 = (f32[4,8,128]{2,1,0:T(8,128)}, f32[4,8,128]{2,1,0:T(8,128)S(1)}, u32[]{:S(2)}, u32[]{:S(2)}) collective-permute-start(f32[4,8,128]{2,1,0:T(8,128)} %get-tuple-element.39.refs_0_), channel_id=1, source_target_pairs={{0,8},{4,12},{8,0},{12,4},{1,9},{5,13},{9,1},{13,5},{2,10},{6,14},... | collective-permute-start | bytes 49160 | tf_op jit(solution)/shard_map/ppermute | solution.py:313
  61.2 5.0 %collective-permute-start.10 = (f32[4,8,128]{2,1,0:T(8,128)}, f32[4,8,128]{2,1,0:T(8,128)S(1)}, u32[]{:S(2)}, u32[]{:S(2)}) collective-permute-start(f32[4,8,128]{2,1,0:T(8,128)} %get-tuple-element.39.refs_0_), channel_id=1, source_target_pairs={{0,12},{4,0},{8,4},{12,8},{1,13},{5,1},{9,5},{13,9},{2,14},{6,2},{... | collective-permute-start | bytes 49160 | tf_op jit(solution)/shard_map/ppermute | solution.py:313
  63.2 5.2 %collective-permute-start.9 = (f32[4,8,128]{2,1,0:T(8,128)}, f32[4,8,128]{2,1,0:T(8,128)S(1)}, u32[]{:S(2)}, u32[]{:S(2)}) collective-permute-start(f32[4,8,128]{2,1,0:T(8,128)} %get-tuple-element.39.refs_0_), channel_id=1, source_target_pairs={{0,4},{4,8},{8,12},{12,0},{1,5},{5,9},{9,13},{13,1},{2,6},{6,10},{... | collective-permute-start | bytes 49160 | tf_op jit(solution)/shard_map/ppermute | solution.py:313
  80.2 26.9 %all-to-all-start.1 = ((bf16[8,224,256]{2,1,0:T(8,128)(2,1)}), bf16[8,224,256]{2,1,0:T(8,128)(2,1)S(1)}, u32[]{:S(2)}, u32[]{:S(2)}) async-start(bf16[8,224,256]{2,1,0:T(8,128)(2,1)} %get-tuple-element.44), calls=%async_computation.1 | async-start | bytes 1835008 | tf_op jit(solution)/shard_map/all_to_all | solution.py:317
  84.2 8.1 %collective-permute-start.12 = (f32[128,512]{1,0:T(8,128)S(1)}, f32[128,512]{1,0:T(8,128)S(1)}, u32[]{:S(2)}, u32[]{:S(2)}) collective-permute-start(f32[128,512]{1,0:T(8,128)S(1)} %get-tuple-element.54), channel_id=1, source_target_pairs={{0,4},{4,8},{8,12},{12,0},{1,5},{5,9},{9,13},{13,1},{2,6},{6,10},{... | collective-permute-start | bytes 786440 | tf_op jit(solution)/shard_map/ppermute | solution.py:313
  84.3 8.2 %collective-permute-start.14 = (f32[128,512]{1,0:T(8,128)S(1)}, f32[128,512]{1,0:T(8,128)S(1)}, u32[]{:S(2)}, u32[]{:S(2)}) collective-permute-start(f32[128,512]{1,0:T(8,128)S(1)} %get-tuple-element.53), channel_id=1, source_target_pairs={{0,12},{4,0},{8,4},{12,8},{1,13},{5,1},{9,5},{13,9},{2,14},{6,2},{... | collective-permute-start | bytes 786440 | tf_op jit(solution)/shard_map/ppermute | solution.py:313
  92.5 18.7 %collective-permute-start.13 = (f32[128,1024]{1,0:T(8,128)S(1)}, f32[128,1024]{1,0:T(8,128)S(1)}, u32[]{:S(2)}, u32[]{:S(2)}) collective-permute-start(f32[128,1024]{1,0:T(8,128)S(1)} %pad_maximum_fusion), channel_id=1, source_target_pairs={{0,4},{4,8},{8,12},{12,0},{1,5},{5,9},{9,13},{13,1},{2,6},{6,10},{... | collective-permute-start | bytes 1572872 | tf_op jit(solution)/shard_map/ppermute | solution.py:313
  93.5 22.8 %copy-start.1 = (f32[128,1024]{1,0:T(8,128)S(1)}, f32[128,1024]{1,0:T(8,128)}, u32[]{:S(2)}) copy-start(f32[128,1024]{1,0:T(8,128)} %get-tuple-element.40.mine) | copy-start | bytes 1572868
  94.4 16.8 %collective-permute-start.15 = (f32[128,1024]{1,0:T(8,128)}, f32[128,1024]{1,0:T(8,128)S(1)}, u32[]{:S(2)}, u32[]{:S(2)}) collective-permute-start(f32[128,1024]{1,0:T(8,128)} %pad_maximum_fusion.1), channel_id=1, source_target_pairs={{0,12},{4,0},{8,4},{12,8},{1,13},{5,1},{9,5},{13,9},{2,14},{6,2},{... | collective-permute-start | bytes 1572872 | tf_op jit(solution)/shard_map/ppermute | solution.py:313
  107.8 8.6 %all-to-all-start.2 = ((f32[8,8,128]{2,1,0:T(8,128)}), f32[8,8,128]{2,1,0:T(8,128)S(1)}, u32[]{:S(2)}, u32[]{:S(2)}) async-start(f32[8,8,128]{2,1,0:T(8,128)} %broadcast_in_dim.52), calls=%async_computation.2 | async-start | bytes 65536 | tf_op jit(solution)/shard_map/all_to_all | solution.py:317
  117.7 11.2 %all-to-all-start.3 = ((bf16[4,48,1024]{2,1,0:T(8,128)(2,1)}), bf16[4,48,1024]{2,1,0:T(8,128)(2,1)S(1)}, u32[]{:S(2)}, u32[]{:S(2)}) async-start(bf16[4,48,1024]{2,1,0:T(8,128)(2,1)} %shard_map.174), calls=%async_computation.3 | async-start | bytes 786432 | tf_op jit(solution)/shard_map/all_to_all | solution.py:317
  (21 other events, 85.1 us)
where the time goes:
time: 132 us; the launch traced here: 130 us
  starting transfers between devices  44.8 us (34%)
  waiting for transfers between devices  44.5 us (34%)
  Pallas kernels  29.6 us (22%)
  local copies, waits for them, and re-layouts  5.15 us (4%)
  other arithmetic  3.34 us (3%)
  between operations  2.84 us (2%)
    pallas_call x6, Pallas kernels, call(): pl.pallas_call(kernel, out_shape=out_shape, in_specs=specs, out_specs=jax...  29.6 us
    ppermute x16, starting transfers between devices, shift(): return lax.ppermute(x, axis, [(i, (i + step) % size) for i in range(size)])  23.9 us
    ppermute x16, waiting for transfers between devices, shift(): return lax.ppermute(x, axis, [(i, (i + step) % size) for i in range(size)])  23 us
    all_to_all x4, waiting for transfers between devices, to_all(): return lax.all_to_all(x, axis, 0, 0, tiled=False)  21.6 us
    all_to_all x4, starting transfers between devices, to_all(): return lax.all_to_all(x, axis, 0, 0, tiled=False)  20.8 us
    unnamed x50, local copies, waits for them, and re-layouts  3.01 us
  transfers between devices with their start and end apart: 20, of which 12 were waited for; matrix products, arithmetic and copies ran while one was open for 2% of the time, Pallas kernels for 6%

commit v1 on v0

--- a/solution.py
+++ b/solution.py
@@ -18,7 +18,7 @@
 Y = 4
 X = 4
 QUARTER = ROWS * Z // 2
-BLOCK = 256
+BLOCK = 512
 PART = TOKENS // X
 PER_ROWS = ROWS // TILE
 PER_PROMPT = PER_ROWS * Y
@@ -251,25 +251,23 @@
     u = unit(kv[:, :HEAD].astype(F32))
     gain_k = gain_k + jnp.sum(scaled * u, axis=0, keepdims=True)
     terms = terms_of(jnp.concatenate([gain_q, gain_k, jnp.zeros((6, HEAD), F32)], axis=0))
-    rows = jnp.concatenate([*terms, jnp.zeros((8, HEAD), BF16)], axis=0)
-    rows = jnp.concatenate([rows, jnp.zeros_like(rows)], axis=1)
+    terms.append(jnp.zeros((8, HEAD), BF16))
+    rows = jnp.concatenate(
+        [jnp.concatenate(terms[:2], axis=0), jnp.concatenate(terms[2:], axis=0)], axis=1
+    )
     for c in range(Z):
         out[c, ROWS:, :] = rows
 
 
-def query_back_kernel(q, qg, mine, left, right, gains, out):
+def query_back_kernel(pos, q, qg, mine, left, right, own, *refs):
+    out, dx = refs[:3], refs[3]
     for j in range(HEADS):
         span = slice(j * HEAD, (j + 1) * HEAD)
         dy = mine[:, span] + left[:, span] + right[:, span]
-        dx = norm_back(q[:, span].astype(F32), qg[...], dy).astype(BF16)
-        for h in range(X):
-            out[h, :PART, span] = dx[h * PART : (h + 1) * PART]
-    terms = terms_of(sum(gains[i] for i in range(2 * Y)))
-    terms.append(jnp.zeros((8, QUERIES - 3 * HEAD), BF16))
-    row = jnp.concatenate(terms, axis=1)
-    row = jnp.concatenate([row, jnp.zeros_like(row)], axis=0)
-    for h in range(X):
-        out[h, PART:, :] = row
+        dx[:, span] = norm_back(q[:, span].astype(F32), qg[...], dy).astype(BF16)
+    for k, ref in enumerate((own, *out)):
+        part = lax.rem(pos[2] + k, X) * PART
+        ref[...] = dx[pl.ds(pl.multiple_of(part, PART), PART), :]
 
 
 def key_back_kernel(k, kg, parts, dk, dv):
@@ -278,13 +276,11 @@
     dv[...] = total[:, HEAD:]
 
 
-def spread_kernel(parts, out, gains):
-    total = jnp.zeros((8, HEAD), F32)
-    for h in range(X):
-        out[:, h * QUERIES : (h + 1) * QUERIES] = parts[h, :PART, :].astype(F32)
-        rows = parts[h, PART:, :].astype(F32)[0:8]
-        total = total + sum(rows[:, i * HEAD : (i + 1) * HEAD] for i in range(3))
-    gains[...] = total
+def spread_kernel(pos, *refs):
+    parts, out = refs[:4], refs[4]
+    for k, ref in enumerate(parts):
+        first = lax.rem(pos[2] + X - k, X) * QUERIES
+        out[:, pl.ds(pl.multiple_of(first, QUERIES), QUERIES)] = ref[...].astype(F32)
 
 
 def call(kernel, out_shape, n_scalar, args, scratch=(), flops=0, nbytes=0, vmem=SMALL):
@@ -307,6 +303,62 @@
 
 def bf16(*shape):
     return jax.ShapeDtypeStruct(shape, BF16)
+
+
+UNIT = 2 * 4 * QUERIES * QUARTER * HEAD
+
+
+def run_stats(pos, info, qg, kg, qs, kv, kr):
+    return call(
+        stats_kernel,
+        (
+            bf16(4, QUERIES, HEAD),
+            bf16(2 * QUARTER, HEAD),
+            bf16(TOKENS, HEAD),
+            f32(Y, 16, 128),
+        ),
+        2,
+        (pos, info, qg, kg, *qs, kv, kr),
+        flops=2 * UNIT,
+        nbytes=1 << 22,
+        vmem=VMEM,
+    )
+
+
+def run_values(pos, info, qh, kh, kv, krh, vr, sts, gos):
+    return call(
+        values_kernel,
+        (
+            bf16(2 * QUARTER, HEAD),
+            f32(TOKENS, HEAD),
+            f32(4, HEADS, 128),
+            f32(Y, HEADS, 128),
+        ),
+        2,
+        (pos, info, qh, kh, kv, krh, vr, *sts, *gos),
+        scratch=[pltpu.VMEM((2 * QUARTER, HEAD), F32)],
+        flops=4 * UNIT,
+        nbytes=1 << 22,
+        vmem=VMEM,
+    )
+
+
+def run_grads(pos, info, lt, qh, kh, kv, krh, vr, kg, kr, dv, dds, gos, qs):
+    return call(
+        grads_kernel,
+        (
+            *[f32(TOKENS, QUERIES)] * 3,
+            f32(2, TOKENS, QUERIES // 2),
+            bf16(Z, ROWS + 16, 2 * HEAD),
+            f32(TOKENS, HEAD),
+        ),
+        2,
+        (pos, info, lt, qh, kh, kv, krh, vr, kg, kr, dv, *dds, *gos, *qs),
+        scratch=[pltpu.VMEM((2, HEAD, QUARTER), BF16), pltpu.VMEM((2 * QUARTER, HEAD), F32)],
+        flops=5 * UNIT,
+        nbytes=1 << 22,
+        vmem=VMEM,
+    )
 
 
 def shift(x, axis, size, step):
@@ -333,7 +385,7 @@
 ):
     y = lax.axis_index("y")
     z = lax.axis_index("z")
-    pos = jnp.stack([y, z]).astype(jnp.int32)
+    pos = jnp.stack([y, z, lax.axis_index("head")]).astype(jnp.int32)
     qg = q_gain[None]
     kg = k_gain[None]
     k_raw = prompt_key_input[0]
@@ -361,54 +413,13 @@
     gos = (go, go_next, go_before, go_far)
     info = jnp.stack([a[TOKENS, :128] for a in qs]).astype(jnp.int32)
 
-    unit_flops = 2 * 4 * QUERIES * QUARTER * HEAD
-    qh, kh, krh, st = call(
-        stats_kernel,
-        (
-            bf16(4, QUERIES, HEAD),
-            bf16(2 * QUARTER, HEAD),
-            bf16(TOKENS, HEAD),
-            f32(Y, 16, 128),
-        ),
-        2,
-        (pos, info, qg, kg, *qs, kv, kr),
-        flops=2 * unit_flops,
-        nbytes=1 << 22,
-        vmem=VMEM,
-    )
+    qh, kh, krh, st = run_stats(pos, info, qg, kg, qs, kv, kr)
     sts = [st] + [shift(st, "y", Y, k) for k in (1, -1, 2)]
-    dv, dvr, lt, dd = call(
-        values_kernel,
-        (
-            bf16(2 * QUARTER, HEAD),
-            f32(TOKENS, HEAD),
-            f32(4, HEADS, 128),
-            f32(Y, HEADS, 128),
-        ),
-        2,
-        (pos, info, qh, kh, kv, krh, vr, *sts, *gos),
-        scratch=[pltpu.VMEM((2 * QUARTER, HEAD), F32)],
-        flops=4 * unit_flops,
-        nbytes=1 << 22,
-        vmem=VMEM,
-    )
+    dv, dvr, lt, dd = run_values(pos, info, qh, kh, kv, krh, vr, sts, gos)
     dds = [dd] + [shift(dd, "y", Y, k) for k in (1, -1, 2)]
-    dq0, dq1, dq2, far, dkv, dkr = call(
-        grads_kernel,
-        (
-            *[f32(TOKENS, QUERIES)] * 3,
-            f32(2, TOKENS, QUERIES // 2),
-            bf16(Z, ROWS + 32, 2 * HEAD),
-            f32(TOKENS, HEAD),
-        ),
-        2,
-        (pos, info, lt, qh, kh, kv, krh, vr, kg, kr, dv, *dds, *gos, *qs),
-        scratch=[pltpu.VMEM((2, HEAD, QUARTER), BF16), pltpu.VMEM((2 * QUARTER, HEAD), F32)],
-        flops=5 * unit_flops,
-        nbytes=1 << 22,
-        vmem=VMEM,
-    )
-
+    dq0, dq1, dq2, far, dkv, dkr = run_grads(
+        pos, info, lt, qh, kh, kv, krh, vr, kg, kr, dv, dds, gos, qs
+    )
     half = QUERIES // 2
     dkvs = to_all(dkv, "z")
     far_up = shift(far[0], "y", Y, 1)
@@ -417,19 +428,22 @@
     to_before = jnp.concatenate([dq2[:, :half], dq2[:, half:] + far_down], axis=1)
     from_before = shift(to_next, "y", Y, 1)
     from_next = shift(to_before, "y", Y, -1)
-    gains = dkvs[:, ROWS : ROWS + 24, :HEAD].astype(F32).reshape(Z * 3, 8, HEAD).sum(axis=0)
-    gains = to_all(jnp.broadcast_to(gains[None], (2 * Y, 8, HEAD)), ("dp", "y"))
-
-    dq = call(
+    rows = dkvs[:, ROWS:, :].astype(F32).sum(axis=0)
+    gains = rows[0:8, :HEAD] + rows[8:16, :HEAD] + rows[0:8, HEAD:]
+    gains = to_all(jnp.broadcast_to(gains[None], (2 * Y * X, 8, HEAD)), ("dp", "y", "head"))
+    gains = gains.sum(axis=0)
+
+    own, *parts = call(
         query_back_kernel,
-        bf16(X, PART + 16, QUERIES),
-        0,
-        (q_raw, qg, dq0, from_before, from_next, gains),
+        (bf16(PART, QUERIES),) * 4,
+        1,
+        (pos, q_raw, qg, dq0, from_before, from_next),
+        scratch=[pltpu.VMEM((TOKENS, QUERIES), BF16)],
         nbytes=1 << 21,
     )
-    dq = to_all(dq, "head")
-    regrouped, gains = call(
-        spread_kernel, (f32(PART, X * QUERIES), f32(8, HEAD)), 0, (dq,), nbytes=1 << 20
+    parts = [own] + [shift(part, "head", X, k + 1) for k, part in enumerate(parts)]
+    regrouped = call(
+        spread_kernel, f32(PART, X * QUERIES), 1, (pos, *parts), nbytes=1 << 20
     )
     dk, dv = call(
         key_back_kernel,

time: 132 us -> 124 us (0.939); the launches traced: 130 us -> 124 us
  waiting for transfers between devices: 44.5 us -> 38 us
    all_to_all x4 -> x3, waiting for transfers between devices: 21.6 us -> 9.61 us  [to_all(): return lax.all_to_all(x, axis, 0, 0, tiled=False)]
    ppermute x16 -> x19, waiting for transfers between devices: 23 us -> 28.4 us  [shift(): return lax.ppermute(x, axis, [(i, (i + step) % size) for i in range(size)])]
    all_to_all x4 -> x3, starting transfers between devices: 20.8 us -> 17.5 us  [to_all(): return lax.all_to_all(x, axis, 0, 0, tiled=False)]
    ppermute x16 -> x19, starting transfers between devices: 23.9 us -> 27 us  [shift(): return lax.ppermute(x, axis, [(i, (i + step) % size) for i in range(size)])]
    unnamed x50 -> x52, local copies, waits for them, and re-layouts: 3.01 us -> 3.65 us
  transfers between devices with their start and end apart: 20 -> 22, of which waited for: 12 -> 13; matrix products, arithmetic and copies ran while one was open for 2% -> 3% of each run, Pallas kernels for 6% -> 8%
where the time goes in v1:
time: 124 us
  starting transfers between devices  44.4 us (36%)
  waiting for transfers between devices  38 us (31%)
  Pallas kernels  29.2 us (24%)
  local copies, waits for them, and re-layouts  5.82 us (5%)
  other arithmetic  3.34 us (3%)
  between operations  2.87 us (2%)
    pallas_call x6, Pallas kernels, call(): pl.pallas_call(kernel, out_shape=out_shape, in_specs=specs, out_specs=jax...  29.2 us
    ppermute x19, waiting for transfers between devices, shift(): return lax.ppermute(x, axis, [(i, (i + step) % size) for i in range(size)])  28.4 us
    ppermute x19, starting transfers between devices, shift(): return lax.ppermute(x, axis, [(i, (i + step) % size) for i in range(size)])  27 us
    all_to_all x3, starting transfers between devices, to_all(): return lax.all_to_all(x, axis, 0, 0, tiled=False)  17.5 us
    all_to_all x3, waiting for transfers between devices, to_all(): return lax.all_to_all(x, axis, 0, 0, tiled=False)  9.61 us
    unnamed x52, local copies, waits for them, and re-layouts  3.65 us
  transfers between devices with their start and end apart: 22, of which 13 were waited for; matrix products, arithmetic and copies ran while one was open for 3% of the time, Pallas kernels for 8%

profile of v1, /device:TPU:6, one launch (start us, length us, event | category | flops | bytes accessed | tf_op | source)
XLA Modules:
  0.0 123.7 jit_solution(5648001013364825846)
XLA Ops:
  2.4 8.6 %all-to-all-start = ((bf16[8,192,256]{2,1,0:T(8,128)(2,1)}), bf16[8,192,256]{2,1,0:T(8,128)(2,1)S(1)}, u32[]{:S(2)}, u32[]{:S(2)}) async-start(bf16[8,192,256]{2,1,0:T(8,128)(2,1)} %broadcast_in_dim.48), calls=%async_computation | async-start | bytes 1572864 | tf_op jit(solution)/shard_map/all_to_all | solution.py:369
  14.1 1.7 %collective-permute-start.1 = (bf16[144,1024]{1,0:T(8,128)(2,1)S(1)}, bf16[144,1024]{1,0:T(8,128)(2,1)S(1)}, u32[]{:S(2)}, u32[]{:S(2)}) collective-permute-start(bf16[144,1024]{1,0:T(8,128)(2,1)S(1)} %pad_maximum_fusion.2.refs_0_.refs_8_), channel_id=1, source_target_pairs={{0,12},{4,0},{8,4},{12,8},{1,13},{5,1},{9,5},{13,9},{2,14},{6,2},{... | collective-permute-start | bytes 884744 | tf_op jit(solution)/shard_map/ppermute | solution.py:365
  17.1 5.2 %collective-permute-done.refs_2_.refs_10_ = bf16[144,1024]{1,0:T(8,128)(2,1)S(1)} collective-permute-done((bf16[144,1024]{1,0:T(8,128)(2,1)S(1)}, bf16[144,1024]{1,0:T(8,128)(2,1)S(1)}, u32[]{:S(2)}, u32[]{:S(2)}) %collective-permute-start) | collective-permute-done | bytes 294944 | tf_op jit(solution)/shard_map/ppermute | solution.py:365
  22.7 3.0 %collective-permute-start.6 = (bf16[128,1024]{1,0:T(8,128)(2,1)S(1)}, bf16[128,1024]{1,0:T(8,128)(2,1)S(1)}, u32[]{:S(2)}, u32[]{:S(2)}) collective-permute-start(bf16[128,1024]{1,0:T(8,128)(2,1)S(1)} %fusion.refs_4_), channel_id=1, source_target_pairs={{0,12},{4,0},{8,4},{12,8},{1,13},{5,1},{9,5},{13,9},{2,14},{6,2},{... | collective-permute-start | bytes 786440 | tf_op jit(solution)/shard_map/ppermute | solution.py:365
  26.3 3.6 %collective-permute-done.6.refs_5_ = bf16[128,1024]{1,0:T(8,128)(2,1)S(1)} collective-permute-done((bf16[128,1024]{1,0:T(8,128)(2,1)S(1)}, bf16[128,1024]{1,0:T(8,128)(2,1)S(1)}, u32[]{:S(2)}, u32[]{:S(2)}) %collective-permute-start.6) | collective-permute-done | bytes 262176 | tf_op jit(solution)/shard_map/ppermute | solution.py:365
  29.9 3.7 %collective-permute-start.8 = (bf16[128,1024]{1,0:T(8,128)(2,1)S(1)}, bf16[128,1024]{1,0:T(8,128)(2,1)S(1)}, u32[]{:S(2)}, u32[]{:S(2)}) collective-permute-start(bf16[128,1024]{1,0:T(8,128)(2,1)S(1)} %collective-permute-done.6.refs_5_), channel_id=1, source_target_pairs={{0,12},{4,0},{8,4},{12,8},{1,13},{5,1},{9,5},{13,9},{2,14},{6,2},{... | collective-permute-start | bytes 786440 | tf_op jit(solution)/shard_map/ppermute | solution.py:365
  35.0 7.1 %shard_map.171 = (bf16[4,1024,128]{2,1,0:T(8,128)(2,1)}, bf16[1536,128]{1,0:T(8,128)(2,1)}, bf16[128,128]{1,0:T(8,128)(2,1)}, f32[4,16,128]{2,1,0:T(8,128)}) custom-call(s32[3]{0:T(128)} %pad_add_fusion.pos, s32[4,128]{1,0:T(4,128)} %maximum_convert_fusion.info, f32[1,128]{1,0:T(1,128)} %bitcast.37, f32[1,128]{1,0:T(1,128)} %bitcast.39, ...), custom_call_target="tpu_custom_call" | custom-call | flops 1610612736 | bytes 4194304 | tf_op jit(solution)/shard_map/pallas_call | solution.py:289
  42.1 3.3 %collective-permute-start.5 = (f32[4,16,128]{2,1,0:T(8,128)}, f32[4,16,128]{2,1,0:T(8,128)S(1)}, u32[]{:S(2)}, u32[]{:S(2)}) collective-permute-start(f32[4,16,128]{2,1,0:T(8,128)} %get-tuple-element.38.refs_0_), channel_id=1, source_target_pairs={{0,8},{4,12},{8,0},{12,4},{1,9},{5,13},{9,1},{13,5},{2,10},{6,14},... | collective-permute-start | bytes 98312 | tf_op jit(solution)/shard_map/ppermute | solution.py:365
  47.8 1.7 %collective-permute-done.4.refs_2_ = f32[4,16,128]{2,1,0:T(8,128)S(1)} collective-permute-done((f32[4,16,128]{2,1,0:T(8,128)}, f32[4,16,128]{2,1,0:T(8,128)S(1)}, u32[]{:S(2)}, u32[]{:S(2)}) %collective-permute-start.4) | collective-permute-done | bytes 32800 | tf_op jit(solution)/shard_map/ppermute | solution.py:365
  49.5 2.3 %collective-permute-done.3.refs_1_ = f32[4,16,128]{2,1,0:T(8,128)S(1)} collective-permute-done((f32[4,16,128]{2,1,0:T(8,128)}, f32[4,16,128]{2,1,0:T(8,128)S(1)}, u32[]{:S(2)}, u32[]{:S(2)}) %collective-permute-start.3) | collective-permute-done | bytes 32800 | tf_op jit(solution)/shard_map/ppermute | solution.py:365
  52.4 8.2 %shard_map.172 = (bf16[1536,128]{1,0:T(8,128)(2,1)}, f32[128,128]{1,0:T(8,128)}, f32[4,8,128]{2,1,0:T(8,128)}, f32[4,8,128]{2,1,0:T(8,128)}) custom-call(s32[3]{0:T(128)} %pad_add_fusion.pos, s32[4,128]{1,0:T(4,128)} %maximum_convert_fusion.info, bf16[4,1024,128]{2,1,0:T(8,128)(2,1)} %get-tuple-element.35.qh, bf16[1536,128]{1,0:T(8,128)(2,1)} %get-tuple-element.36.kh, ...), custom_call_target="tpu_custom_call" | custom-call | flops 3221225472 | bytes 4194304 | tf_op jit(solution)/shard_map/pallas_call | solution.py:289
  61.2 1.9 %collective-permute-start.10 = (f32[4,8,128]{2,1,0:T(8,128)}, f32[4,8,128]{2,1,0:T(8,128)S(1)}, u32[]{:S(2)}, u32[]{:S(2)}) collective-permute-start(f32[4,8,128]{2,1,0:T(8,128)} %get-tuple-element.41.refs_0_), channel_id=1, source_target_pairs={{0,12},{4,0},{8,4},{12,8},{1,13},{5,1},{9,5},{13,9},{2,14},{6,2},{... | collective-permute-start | bytes 49160 | tf_op jit(solution)/shard_map/ppermute | solution.py:365
  63.2 2.9 %collective-permute-done.11.refs_3_ = f32[4,8,128]{2,1,0:T(8,128)S(1)} collective-permute-done((f32[4,8,128]{2,1,0:T(8,128)}, f32[4,8,128]{2,1,0:T(8,128)S(1)}, u32[]{:S(2)}, u32[]{:S(2)}) %collective-permute-start.11) | collective-permute-done | bytes 16416 | tf_op jit(solution)/shard_map/ppermute | solution.py:365
  66.1 2.1 %collective-permute-done.9.refs_1_ = f32[4,8,128]{2,1,0:T(8,128)S(1)} collective-permute-done((f32[4,8,128]{2,1,0:T(8,128)}, f32[4,8,128]{2,1,0:T(8,128)S(1)}, u32[]{:S(2)}, u32[]{:S(2)}) %collective-permute-start.9) | collective-permute-done | bytes 16416 | tf_op jit(solution)/shard_map/ppermute | solution.py:365
  68.9 10.5 %shard_map.173 = (f32[128,1024]{1,0:T(8,128)}, f32[128,1024]{1,0:T(8,128)}, f32[128,1024]{1,0:T(8,128)}, f32[2,128,512]{2,1,0:T(8,128)}, bf16[8,208,256]{2,1,0:T(8,128)(2,1)}, /*index=5*/f32[128,128]{1,0:T(8,128)}) custom-call(s32[3]{0:T(128)} %pad_add_fusion.pos, s32[4,128]{1,0:T(4,128)} %maximum_convert_fusion.info, f32[4,8,128]{2,1,0:T(8,128)} %get-tuple-element.39.lt, ...), custom_call_target="tpu_custom_call" | custom-call | flops 4026531840 | bytes 4194304 | tf_op jit(solution)/shard_map/pallas_call | solution.py:289
  79.4 4.0 %all-to-all-start.1 = ((bf16[8,208,256]{2,1,0:T(8,128)(2,1)}), bf16[8,208,256]{2,1,0:T(8,128)(2,1)S(1)}, u32[]{:S(2)}, u32[]{:S(2)}) async-start(bf16[8,208,256]{2,1,0:T(8,128)(2,1)} %get-tuple-element.52), calls=%async_computation.1 | async-start | bytes 1703936 | tf_op jit(solution)/shard_map/all_to_all | solution.py:369
  83.5 3.2 %collective-permute-start.14 = (f32[128,512]{1,0:T(8,128)S(1)}, f32[128,512]{1,0:T(8,128)S(1)}, u32[]{:S(2)}, u32[]{:S(2)}) collective-permute-start(f32[128,512]{1,0:T(8,128)S(1)} %get-tuple-element.57), channel_id=1, source_target_pairs={{0,12},{4,0},{8,4},{12,8},{1,13},{5,1},{9,5},{13,9},{2,14},{6,2},{... | collective-permute-start | bytes 786440 | tf_op jit(solution)/shard_map/ppermute | solution.py:365
  86.8 4.8 %collective-permute-done.12 = f32[128,512]{1,0:T(8,128)S(1)} collective-permute-done((f32[128,512]{1,0:T(8,128)S(1)}, f32[128,512]{1,0:T(8,128)S(1)}, u32[]{:S(2)}, u32[]{:S(2)}) %collective-permute-start.12) | collective-permute-done | bytes 262176 | tf_op jit(solution)/shard_map/ppermute | solution.py:365
  93.6 2.3 %collective-permute-start.15 = (f32[128,1024]{1,0:T(8,128)}, f32[128,1024]{1,0:T(8,128)S(1)}, u32[]{:S(2)}, u32[]{:S(2)}) collective-permute-start(f32[128,1024]{1,0:T(8,128)} %pad_maximum_fusion.1), channel_id=1, source_target_pairs={{0,12},{4,0},{8,4},{12,8},{1,13},{5,1},{9,5},{13,9},{2,14},{6,2},{... | collective-permute-start | bytes 1572872 | tf_op jit(solution)/shard_map/ppermute | solution.py:365
  95.9 9.1 %all-to-all-done.1.parts = bf16[8,208,256]{2,1,0:T(8,128)(2,1)S(1)} async-done(((bf16[8,208,256]{2,1,0:T(8,128)(2,1)}), bf16[8,208,256]{2,1,0:T(8,128)(2,1)S(1)}, u32[]{:S(2)}, u32[]{:S(2)}) %all-to-all-start.1) | async-done | bytes 852000 | tf_op jit(solution)/shard_map/all_to_all | solution.py:369
  105.7 4.9 %all-to-all-start.2 = ((f32[32,8,128]{2,1,0:T(8,128)}), f32[32,8,128]{2,1,0:T(8,128)S(1)}, u32[]{:S(2)}, u32[]{:S(2)}) async-start(f32[32,8,128]{2,1,0:T(8,128)} %broadcast_in_dim.57), calls=%async_computation.2 | async-start | bytes 262144 | tf_op jit(solution)/shard_map/all_to_all | solution.py:369
  112.7 2.7 %collective-permute-start.17 = (bf16[32,1024]{1,0:T(8,128)(2,1)S(1)}, bf16[32,1024]{1,0:T(8,128)(2,1)S(1)}, u32[]{:S(2)}, u32[]{:S(2)}) collective-permute-start(bf16[32,1024]{1,0:T(8,128)(2,1)S(1)} %get-tuple-element.48), channel_id=1, source_target_pairs={{0,2},{1,3},{2,0},{3,1},{4,6},{5,7},{6,4},{7,5},{8,10},{9,11},{10,... | collective-permute-start | bytes 196616 | tf_op jit(solution)/shard_map/ppermute | solution.py:365
  115.4 1.9 %collective-permute-done.16.refs_1_ = bf16[32,1024]{1,0:T(8,128)(2,1)S(1)} collective-permute-done((bf16[32,1024]{1,0:T(8,128)(2,1)S(1)}, bf16[32,1024]{1,0:T(8,128)(2,1)S(1)}, u32[]{:S(2)}, u32[]{:S(2)}) %collective-permute-start.16) | collective-permute-done | bytes 65568 | tf_op jit(solution)/shard_map/ppermute | solution.py:365
  118.5 2.4 %collective-permute-done.18.refs_3_ = bf16[32,1024]{1,0:T(8,128)(2,1)S(1)} collective-permute-done((bf16[32,1024]{1,0:T(8,128)(2,1)S(1)}, bf16[32,1024]{1,0:T(8,128)(2,1)S(1)}, u32[]{:S(2)}, u32[]{:S(2)}) %collective-permute-start.18) | collective-permute-done | bytes 65568 | tf_op jit(solution)/shard_map/ppermute | solution.py:365
  (101 shorter events, 19.8 us)
Async XLA Ops:
  2.4 31.7 %all-to-all-start = ((bf16[8,192,256]{2,1,0:T(8,128)(2,1)}), bf16[8,192,256]{2,1,0:T(8,128)(2,1)S(1)}, u32[]{:S(2)}, u32[]{:S(2)}) async-start(bf16[8,192,256]{2,1,0:T(8,128)(2,1)} %broadcast_in_dim.48), calls=%async_computation | async-start | bytes 1572864 | tf_op jit(solution)/shard_map/all_to_all | solution.py:369
  12.4 22.4 %copy-start.10 = (bf16[144,1024]{1,0:T(8,128)(2,1)}, bf16[144,1024]{1,0:T(8,128)(2,1)S(1)}, u32[]{:S(2)}) copy-start(bf16[144,1024]{1,0:T(8,128)(2,1)S(1)} %pad_maximum_fusion.2.refs_0_.refs_8_) | copy-start | bytes 884740
  12.4 9.8 %collective-permute-start = (bf16[144,1024]{1,0:T(8,128)(2,1)S(1)}, bf16[144,1024]{1,0:T(8,128)(2,1)S(1)}, u32[]{:S(2)}, u32[]{:S(2)}) collective-permute-start(bf16[144,1024]{1,0:T(8,128)(2,1)S(1)} %pad_maximum_fusion.2.refs_0_.refs_8_), channel_id=1, source_target_pairs={{0,4},{4,8},{8,12},{12,0},{1,5},{5,9},{9,13},{13,1},{2,6},{6,10},{... | collective-permute-start | bytes 884744 | tf_op jit(solution)/shard_map/ppermute | solution.py:365
  14.1 19.5 %collective-permute-start.1 = (bf16[144,1024]{1,0:T(8,128)(2,1)S(1)}, bf16[144,1024]{1,0:T(8,128)(2,1)S(1)}, u32[]{:S(2)}, u32[]{:S(2)}) collective-permute-start(bf16[144,1024]{1,0:T(8,128)(2,1)S(1)} %pad_maximum_fusion.2.refs_0_.refs_8_), channel_id=1, source_target_pairs={{0,12},{4,0},{8,4},{12,8},{1,13},{5,1},{9,5},{13,9},{2,14},{6,2},{... | collective-permute-start | bytes 884744 | tf_op jit(solution)/shard_map/ppermute | solution.py:365
  22.3 11.3 %collective-permute-start.2 = (bf16[144,1024]{1,0:T(8,128)(2,1)S(1)}, bf16[144,1024]{1,0:T(8,128)(2,1)S(1)}, u32[]{:S(2)}, u32[]{:S(2)}) collective-permute-start(bf16[144,1024]{1,0:T(8,128)(2,1)S(1)} %collective-permute-done.refs_2_.refs_10_), channel_id=1, source_target_pairs={{0,4},{4,8},{8,12},{12,0},{1,5},{5,9},{9,13},{13,1},{2,6},{6,10},{... | collective-permute-start | bytes 884744 | tf_op jit(solution)/shard_map/ppermute | solution.py:365
  22.7 19.4 %copy-start.12 = (bf16[128,1024]{1,0:T(8,128)(2,1)}, bf16[128,1024]{1,0:T(8,128)(2,1)S(1)}, u32[]{:S(2)}) copy-start(bf16[128,1024]{1,0:T(8,128)(2,1)S(1)} %fusion.refs_4_) | copy-start | bytes 786436
  22.7 7.2 %collective-permute-start.6 = (bf16[128,1024]{1,0:T(8,128)(2,1)S(1)}, bf16[128,1024]{1,0:T(8,128)(2,1)S(1)}, u32[]{:S(2)}, u32[]{:S(2)}) collective-permute-start(bf16[128,1024]{1,0:T(8,128)(2,1)S(1)} %fusion.refs_4_), channel_id=1, source_target_pairs={{0,12},{4,0},{8,4},{12,8},{1,13},{5,1},{9,5},{13,9},{2,14},{6,2},{... | collective-permute-start | bytes 786440 | tf_op jit(solution)/shard_map/ppermute | solution.py:365
  25.7 21.7 %collective-permute-start.7 = (bf16[128,1024]{1,0:T(8,128)(2,1)S(1)}, bf16[128,1024]{1,0:T(8,128)(2,1)S(1)}, u32[]{:S(2)}, u32[]{:S(2)}) collective-permute-start(bf16[128,1024]{1,0:T(8,128)(2,1)S(1)} %fusion.refs_4_), channel_id=1, source_target_pairs={{0,4},{4,8},{8,12},{12,0},{1,5},{5,9},{9,13},{13,1},{2,6},{6,10},{... | collective-permute-start | bytes 786440 | tf_op jit(solution)/shard_map/ppermute | solution.py:365
  29.9 17.6 %collective-permute-start.8 = (bf16[128,1024]{1,0:T(8,128)(2,1)S(1)}, bf16[128,1024]{1,0:T(8,128)(2,1)S(1)}, u32[]{:S(2)}, u32[]{:S(2)}) collective-permute-start(bf16[128,1024]{1,0:T(8,128)(2,1)S(1)} %collective-permute-done.6.refs_5_), channel_id=1, source_target_pairs={{0,12},{4,0},{8,4},{12,8},{1,13},{5,1},{9,5},{13,9},{2,14},{6,2},{... | collective-permute-start | bytes 786440 | tf_op jit(solution)/shard_map/ppermute | solution.py:365
  42.1 5.7 %collective-permute-start.5 = (f32[4,16,128]{2,1,0:T(8,128)}, f32[4,16,128]{2,1,0:T(8,128)S(1)}, u32[]{:S(2)}, u32[]{:S(2)}) collective-permute-start(f32[4,16,128]{2,1,0:T(8,128)} %get-tuple-element.38.refs_0_), channel_id=1, source_target_pairs={{0,8},{4,12},{8,0},{12,4},{1,9},{5,13},{9,1},{13,5},{2,10},{6,14},... | collective-permute-start | bytes 98312 | tf_op jit(solution)/shard_map/ppermute | solution.py:365
  45.4 4.1 %collective-permute-start.4 = (f32[4,16,128]{2,1,0:T(8,128)}, f32[4,16,128]{2,1,0:T(8,128)S(1)}, u32[]{:S(2)}, u32[]{:S(2)}) collective-permute-start(f32[4,16,128]{2,1,0:T(8,128)} %get-tuple-element.38.refs_0_), channel_id=1, source_target_pairs={{0,12},{4,0},{8,4},{12,8},{1,13},{5,1},{9,5},{13,9},{2,14},{6,2},{... | collective-permute-start | bytes 98312 | tf_op jit(solution)/shard_map/ppermute | solution.py:365
  46.4 5.3 %collective-permute-start.3 = (f32[4,16,128]{2,1,0:T(8,128)}, f32[4,16,128]{2,1,0:T(8,128)S(1)}, u32[]{:S(2)}, u32[]{:S(2)}) collective-permute-start(f32[4,16,128]{2,1,0:T(8,128)} %get-tuple-element.38.refs_0_), channel_id=1, source_target_pairs={{0,4},{4,8},{8,12},{12,0},{1,5},{5,9},{9,13},{13,1},{2,6},{6,10},{... | collective-permute-start | bytes 98312 | tf_op jit(solution)/shard_map/ppermute | solution.py:365
  60.6 5.5 %collective-permute-start.11 = (f32[4,8,128]{2,1,0:T(8,128)}, f32[4,8,128]{2,1,0:T(8,128)S(1)}, u32[]{:S(2)}, u32[]{:S(2)}) collective-permute-start(f32[4,8,128]{2,1,0:T(8,128)} %get-tuple-element.41.refs_0_), channel_id=1, source_target_pairs={{0,8},{4,12},{8,0},{12,4},{1,9},{5,13},{9,1},{13,5},{2,10},{6,14},... | collective-permute-start | bytes 49160 | tf_op jit(solution)/shard_map/ppermute | solution.py:365
  61.2 5.0 %collective-permute-start.10 = (f32[4,8,128]{2,1,0:T(8,128)}, f32[4,8,128]{2,1,0:T(8,128)S(1)}, u32[]{:S(2)}, u32[]{:S(2)}) collective-permute-start(f32[4,8,128]{2,1,0:T(8,128)} %get-tuple-element.41.refs_0_), channel_id=1, source_target_pairs={{0,12},{4,0},{8,4},{12,8},{1,13},{5,1},{9,5},{13,9},{2,14},{6,2},{... | collective-permute-start | bytes 49160 | tf_op jit(solution)/shard_map/ppermute | solution.py:365
  63.1 5.2 %collective-permute-start.9 = (f32[4,8,128]{2,1,0:T(8,128)}, f32[4,8,128]{2,1,0:T(8,128)S(1)}, u32[]{:S(2)}, u32[]{:S(2)}) collective-permute-start(f32[4,8,128]{2,1,0:T(8,128)} %get-tuple-element.41.refs_0_), channel_id=1, source_target_pairs={{0,4},{4,8},{8,12},{12,0},{1,5},{5,9},{9,13},{13,1},{2,6},{6,10},{... | collective-permute-start | bytes 49160 | tf_op jit(solution)/shard_map/ppermute | solution.py:365
  79.4 25.5 %all-to-all-start.1 = ((bf16[8,208,256]{2,1,0:T(8,128)(2,1)}), bf16[8,208,256]{2,1,0:T(8,128)(2,1)S(1)}, u32[]{:S(2)}, u32[]{:S(2)}) async-start(bf16[8,208,256]{2,1,0:T(8,128)(2,1)} %get-tuple-element.52), calls=%async_computation.1 | async-start | bytes 1703936 | tf_op jit(solution)/shard_map/all_to_all | solution.py:369
  83.5 8.1 %collective-permute-start.12 = (f32[128,512]{1,0:T(8,128)S(1)}, f32[128,512]{1,0:T(8,128)S(1)}, u32[]{:S(2)}, u32[]{:S(2)}) collective-permute-start(f32[128,512]{1,0:T(8,128)S(1)} %get-tuple-element.58), channel_id=1, source_target_pairs={{0,4},{4,8},{8,12},{12,0},{1,5},{5,9},{9,13},{13,1},{2,6},{6,10},{... | collective-permute-start | bytes 786440 | tf_op jit(solution)/shard_map/ppermute | solution.py:365
  83.5 8.2 %collective-permute-start.14 = (f32[128,512]{1,0:T(8,128)S(1)}, f32[128,512]{1,0:T(8,128)S(1)}, u32[]{:S(2)}, u32[]{:S(2)}) collective-permute-start(f32[128,512]{1,0:T(8,128)S(1)} %get-tuple-element.57), channel_id=1, source_target_pairs={{0,12},{4,0},{8,4},{12,8},{1,13},{5,1},{9,5},{13,9},{2,14},{6,2},{... | collective-permute-start | bytes 786440 | tf_op jit(solution)/shard_map/ppermute | solution.py:365
  91.7 19.0 %collective-permute-start.13 = (f32[128,1024]{1,0:T(8,128)S(1)}, f32[128,1024]{1,0:T(8,128)S(1)}, u32[]{:S(2)}, u32[]{:S(2)}) collective-permute-start(f32[128,1024]{1,0:T(8,128)S(1)} %pad_maximum_fusion), channel_id=1, source_target_pairs={{0,4},{4,8},{8,12},{12,0},{1,5},{5,9},{9,13},{13,1},{2,6},{6,10},{... | collective-permute-start | bytes 1572872 | tf_op jit(solution)/shard_map/ppermute | solution.py:365
  93.6 17.1 %collective-permute-start.15 = (f32[128,1024]{1,0:T(8,128)}, f32[128,1024]{1,0:T(8,128)S(1)}, u32[]{:S(2)}, u32[]{:S(2)}) collective-permute-start(f32[128,1024]{1,0:T(8,128)} %pad_maximum_fusion.1), channel_id=1, source_target_pairs={{0,12},{4,0},{8,4},{12,8},{1,13},{5,1},{9,5},{13,9},{2,14},{6,2},{... | collective-permute-start | bytes 1572872 | tf_op jit(solution)/shard_map/ppermute | solution.py:365
  105.7 17.5 %all-to-all-start.2 = ((f32[32,8,128]{2,1,0:T(8,128)}), f32[32,8,128]{2,1,0:T(8,128)S(1)}, u32[]{:S(2)}, u32[]{:S(2)}) async-start(f32[32,8,128]{2,1,0:T(8,128)} %broadcast_in_dim.57), calls=%async_computation.2 | async-start | bytes 262144 | tf_op jit(solution)/shard_map/all_to_all | solution.py:369
  112.4 4.9 %collective-permute-start.16 = (bf16[32,1024]{1,0:T(8,128)(2,1)S(1)}, bf16[32,1024]{1,0:T(8,128)(2,1)S(1)}, u32[]{:S(2)}, u32[]{:S(2)}) collective-permute-start(bf16[32,1024]{1,0:T(8,128)(2,1)S(1)} %get-tuple-element.47), channel_id=1, source_target_pairs={{0,1},{1,2},{2,3},{3,0},{4,5},{5,6},{6,7},{7,4},{8,9},{9,10},{10,1... | collective-permute-start | bytes 196616 | tf_op jit(solution)/shard_map/ppermute | solution.py:365
  112.7 5.8 %collective-permute-start.17 = (bf16[32,1024]{1,0:T(8,128)(2,1)S(1)}, bf16[32,1024]{1,0:T(8,128)(2,1)S(1)}, u32[]{:S(2)}, u32[]{:S(2)}) collective-permute-start(bf16[32,1024]{1,0:T(8,128)(2,1)S(1)} %get-tuple-element.48), channel_id=1, source_target_pairs={{0,2},{1,3},{2,0},{3,1},{4,6},{5,7},{6,4},{7,5},{8,10},{9,11},{10,... | collective-permute-start | bytes 196616 | tf_op jit(solution)/shard_map/ppermute | solution.py:365
  115.4 5.5 %collective-permute-start.18 = (bf16[32,1024]{1,0:T(8,128)(2,1)S(1)}, bf16[32,1024]{1,0:T(8,128)(2,1)S(1)}, u32[]{:S(2)}, u32[]{:S(2)}) collective-permute-start(bf16[32,1024]{1,0:T(8,128)(2,1)S(1)} %get-tuple-element.49), channel_id=1, source_target_pairs={{0,3},{1,0},{2,1},{3,2},{4,7},{5,4},{6,5},{7,6},{8,11},{9,8},{10,9... | collective-permute-start | bytes 196616 | tf_op jit(solution)/shard_map/ppermute | solution.py:365
  (24 other events, 104.5 us)

commit v2 on v1

--- a/solution.py
+++ b/solution.py
@@ -26,7 +26,7 @@
 NEGATIVE = -1e30
 SCALE = HEAD ** (-0.5)
 SCALE2 = SCALE * 1.4426950408889634
-VMEM = 56 * 1024 * 1024
+VMEM = 50 * 1024 * 1024
 SMALL = 12 * 1024 * 1024
 F32 = jnp.float32
 BF16 = jnp.bfloat16

time: 124 us -> 121 us (0.976)
  Pallas kernels: 29.2 us -> 25.4 us
    pallas_call x6, Pallas kernels: 29.2 us -> 25.4 us  [call(): pl.pallas_call(kernel, out_shape=out_shape, in_specs=specs, out_specs=jax...]
    unnamed x52 -> x34, local copies, waits for them, and re-layouts: 3.65 us -> 4.21 us
  transfers between devices with their start and end apart: 22 -> 22, of which waited for: 13 -> 13; matrix products, arithmetic and copies ran while one was open for 3% -> 2% of each run, Pallas kernels for 8% -> 7%
where the time goes in v2:
time: 121 us; the launch traced here: 120 us
  starting transfers between devices  44.4 us (37%)
  waiting for transfers between devices  38.3 us (32%)
  Pallas kernels  25.4 us (21%)
  local copies, waits for them, and re-layouts  6.39 us (5%)
  other arithmetic  3.07 us (3%)
  between operations  2.82 us (2%)
    ppermute x19, waiting for transfers between devices, shift(): return lax.ppermute(x, axis, [(i, (i + step) % size) for i in range(size)])  28.5 us
    ppermute x19, starting transfers between devices, shift(): return lax.ppermute(x, axis, [(i, (i + step) % size) for i in range(size)])  27 us
    pallas_call x6, Pallas kernels, call(): pl.pallas_call(kernel, out_shape=out_shape, in_specs=specs, out_specs=jax...  25.4 us
    all_to_all x3, starting transfers between devices, to_all(): return lax.all_to_all(x, axis, 0, 0, tiled=False)  17.5 us
    all_to_all x3, waiting for transfers between devices, to_all(): return lax.all_to_all(x, axis, 0, 0, tiled=False)  9.81 us
    unnamed x34, local copies, waits for them, and re-layouts  4.21 us
  transfers between devices with their start and end apart: 22, of which 13 were waited for; matrix products, arithmetic and copies ran while one was open for 2% of the time, Pallas kernels for 7%

profile of v2, /device:TPU:6, one launch (start us, length us, event | category | flops | bytes accessed | tf_op | source)
XLA Modules:
  0.0 120.4 jit_solution(3998595285515633665)
XLA Ops:
  2.4 8.6 %all-to-all-start = ((bf16[8,192,256]{2,1,0:T(8,128)(2,1)}), bf16[8,192,256]{2,1,0:T(8,128)(2,1)S(1)}, u32[]{:S(2)}, u32[]{:S(2)}) async-start(bf16[8,192,256]{2,1,0:T(8,128)(2,1)} %broadcast_in_dim.48), calls=%async_computation | async-start | bytes 1572864 | tf_op jit(solution)/shard_map/all_to_all | solution.py:369
  14.1 1.7 %collective-permute-start.1 = (bf16[144,1024]{1,0:T(8,128)(2,1)S(1)}, bf16[144,1024]{1,0:T(8,128)(2,1)S(1)}, u32[]{:S(2)}, u32[]{:S(2)}) collective-permute-start(bf16[144,1024]{1,0:T(8,128)(2,1)S(1)} %pad_maximum_fusion.2.refs_0_.refs_8_), channel_id=1, source_target_pairs={{0,12},{4,0},{8,4},{12,8},{1,13},{5,1},{9,5},{13,9},{2,14},{6,2},{... | collective-permute-start | bytes 884744 | tf_op jit(solution)/shard_map/ppermute | solution.py:365
  17.1 5.2 %collective-permute-done.refs_2_.refs_10_ = bf16[144,1024]{1,0:T(8,128)(2,1)S(1)} collective-permute-done((bf16[144,1024]{1,0:T(8,128)(2,1)S(1)}, bf16[144,1024]{1,0:T(8,128)(2,1)S(1)}, u32[]{:S(2)}, u32[]{:S(2)}) %collective-permute-start) | collective-permute-done | bytes 294944 | tf_op jit(solution)/shard_map/ppermute | solution.py:365
  22.7 3.0 %collective-permute-start.6 = (bf16[128,1024]{1,0:T(8,128)(2,1)S(1)}, bf16[128,1024]{1,0:T(8,128)(2,1)S(1)}, u32[]{:S(2)}, u32[]{:S(2)}) collective-permute-start(bf16[128,1024]{1,0:T(8,128)(2,1)S(1)} %fusion.refs_4_), channel_id=1, source_target_pairs={{0,12},{4,0},{8,4},{12,8},{1,13},{5,1},{9,5},{13,9},{2,14},{6,2},{... | collective-permute-start | bytes 786440 | tf_op jit(solution)/shard_map/ppermute | solution.py:365
  25.8 4.1 %collective-permute-done.6.refs_5_ = bf16[128,1024]{1,0:T(8,128)(2,1)S(1)} collective-permute-done((bf16[128,1024]{1,0:T(8,128)(2,1)S(1)}, bf16[128,1024]{1,0:T(8,128)(2,1)S(1)}, u32[]{:S(2)}, u32[]{:S(2)}) %collective-permute-start.6) | collective-permute-done | bytes 262176 | tf_op jit(solution)/shard_map/ppermute | solution.py:365
  29.9 3.7 %collective-permute-start.8 = (bf16[128,1024]{1,0:T(8,128)(2,1)S(1)}, bf16[128,1024]{1,0:T(8,128)(2,1)S(1)}, u32[]{:S(2)}, u32[]{:S(2)}) collective-permute-start(bf16[128,1024]{1,0:T(8,128)(2,1)S(1)} %collective-permute-done.6.refs_5_), channel_id=1, source_target_pairs={{0,12},{4,0},{8,4},{12,8},{1,13},{5,1},{9,5},{13,9},{2,14},{6,2},{... | collective-permute-start | bytes 786440 | tf_op jit(solution)/shard_map/ppermute | solution.py:365
  34.9 5.6 %shard_map.171 = (bf16[4,1024,128]{2,1,0:T(8,128)(2,1)S(1)}, bf16[1536,128]{1,0:T(8,128)(2,1)S(1)}, bf16[128,128]{1,0:T(8,128)(2,1)S(1)}, f32[4,16,128]{2,1,0:T(8,128)S(1)}) custom-call(s32[3]{0:T(128)S(1)} %pad_add_fusion.pos, s32[4,128]{1,0:T(4,128)S(1)} %maximum_convert_fusion.info, f32[1,128]{1,0:T(1,128)S(1)} %bitcast.40, f32[1,128]{1,0:T(1,128)S(1)} %bitcast.42, ...), custom_call_target="tpu_custom_call" | custom-call | flops 1610612736 | bytes 4194304 | tf_op jit(solution)/shard_map/pallas_call | solution.py:289
  40.5 3.3 %collective-permute-start.5 = (f32[4,16,128]{2,1,0:T(8,128)S(1)}, f32[4,16,128]{2,1,0:T(8,128)S(1)}, u32[]{:S(2)}, u32[]{:S(2)}) collective-permute-start(f32[4,16,128]{2,1,0:T(8,128)S(1)} %get-tuple-element.38.refs_0_), channel_id=1, source_target_pairs={{0,8},{4,12},{8,0},{12,4},{1,9},{5,13},{9,1},{13,5},{2,10},{6,14},... | collective-permute-start | bytes 98312 | tf_op jit(solution)/shard_map/ppermute | solution.py:365
  46.0 1.7 %collective-permute-done.4.refs_2_ = f32[4,16,128]{2,1,0:T(8,128)S(1)} collective-permute-done((f32[4,16,128]{2,1,0:T(8,128)S(1)}, f32[4,16,128]{2,1,0:T(8,128)S(1)}, u32[]{:S(2)}, u32[]{:S(2)}) %collective-permute-start.4) | collective-permute-done | bytes 32800 | tf_op jit(solution)/shard_map/ppermute | solution.py:365
  47.7 2.3 %collective-permute-done.3.refs_1_ = f32[4,16,128]{2,1,0:T(8,128)S(1)} collective-permute-done((f32[4,16,128]{2,1,0:T(8,128)S(1)}, f32[4,16,128]{2,1,0:T(8,128)S(1)}, u32[]{:S(2)}, u32[]{:S(2)}) %collective-permute-start.3) | collective-permute-done | bytes 32800 | tf_op jit(solution)/shard_map/ppermute | solution.py:365
  50.0 6.5 %shard_map.172 = (bf16[1536,128]{1,0:T(8,128)(2,1)S(1)}, f32[128,128]{1,0:T(8,128)}, f32[4,8,128]{2,1,0:T(8,128)S(1)}, f32[4,8,128]{2,1,0:T(8,128)S(1)}) custom-call(s32[3]{0:T(128)S(1)} %pad_add_fusion.pos, s32[4,128]{1,0:T(4,128)S(1)} %maximum_convert_fusion.info, bf16[4,1024,128]{2,1,0:T(8,128)(2,1)S(1)} %get-tuple-element.35.qh, ...), custom_call_target="tpu_custom_call" | custom-call | flops 3221225472 | bytes 4194304 | tf_op jit(solution)/shard_map/pallas_call | solution.py:289
  57.1 1.9 %collective-permute-start.10 = (f32[4,8,128]{2,1,0:T(8,128)S(1)}, f32[4,8,128]{2,1,0:T(8,128)S(1)}, u32[]{:S(2)}, u32[]{:S(2)}) collective-permute-start(f32[4,8,128]{2,1,0:T(8,128)S(1)} %get-tuple-element.41.refs_0_), channel_id=1, source_target_pairs={{0,12},{4,0},{8,4},{12,8},{1,13},{5,1},{9,5},{13,9},{2,14},{6,2},{... | collective-permute-start | bytes 49160 | tf_op jit(solution)/shard_map/ppermute | solution.py:365
  59.1 2.7 %collective-permute-done.11.refs_3_ = f32[4,8,128]{2,1,0:T(8,128)S(1)} collective-permute-done((f32[4,8,128]{2,1,0:T(8,128)S(1)}, f32[4,8,128]{2,1,0:T(8,128)S(1)}, u32[]{:S(2)}, u32[]{:S(2)}) %collective-permute-start.11) | collective-permute-done | bytes 16416 | tf_op jit(solution)/shard_map/ppermute | solution.py:365
  61.8 2.1 %collective-permute-done.9.refs_1_ = f32[4,8,128]{2,1,0:T(8,128)S(1)} collective-permute-done((f32[4,8,128]{2,1,0:T(8,128)S(1)}, f32[4,8,128]{2,1,0:T(8,128)S(1)}, u32[]{:S(2)}, u32[]{:S(2)}) %collective-permute-start.9) | collective-permute-done | bytes 16416 | tf_op jit(solution)/shard_map/ppermute | solution.py:365
  65.9 9.9 %shard_map.173 = (f32[128,1024]{1,0:T(8,128)S(1)}, f32[128,1024]{1,0:T(8,128)}, f32[128,1024]{1,0:T(8,128)}, f32[2,128,512]{2,1,0:T(8,128)}, bf16[8,208,256]{2,1,0:T(8,128)(2,1)}, /*index=5*/f32[128,128]{1,0:T(8,128)}) custom-call(s32[3]{0:T(128)S(1)} %pad_add_fusion.pos, s32[4,128]{1,0:T(4,128)S(1)} %maximum_convert_fusion.info, ...), custom_call_target="tpu_custom_call" | custom-call | flops 4026531840 | bytes 4194304 | tf_op jit(solution)/shard_map/pallas_call | solution.py:289
  75.8 3.9 %all-to-all-start.1 = ((bf16[8,208,256]{2,1,0:T(8,128)(2,1)}), bf16[8,208,256]{2,1,0:T(8,128)(2,1)S(1)}, u32[]{:S(2)}, u32[]{:S(2)}) async-start(bf16[8,208,256]{2,1,0:T(8,128)(2,1)} %get-tuple-element.52), calls=%async_computation.1 | async-start | bytes 1703936 | tf_op jit(solution)/shard_map/all_to_all | solution.py:369
  79.8 3.2 %collective-permute-start.14 = (f32[128,512]{1,0:T(8,128)S(1)}, f32[128,512]{1,0:T(8,128)S(1)}, u32[]{:S(2)}, u32[]{:S(2)}) collective-permute-start(f32[128,512]{1,0:T(8,128)S(1)} %get-tuple-element.57), channel_id=1, source_target_pairs={{0,12},{4,0},{8,4},{12,8},{1,13},{5,1},{9,5},{13,9},{2,14},{6,2},{... | collective-permute-start | bytes 786440 | tf_op jit(solution)/shard_map/ppermute | solution.py:365
  83.0 4.7 %collective-permute-done.12 = f32[128,512]{1,0:T(8,128)S(1)} collective-permute-done((f32[128,512]{1,0:T(8,128)S(1)}, f32[128,512]{1,0:T(8,128)S(1)}, u32[]{:S(2)}, u32[]{:S(2)}) %collective-permute-start.12) | collective-permute-done | bytes 262176 | tf_op jit(solution)/shard_map/ppermute | solution.py:365
  89.7 2.3 %collective-permute-start.15 = (f32[128,1024]{1,0:T(8,128)}, f32[128,1024]{1,0:T(8,128)S(1)}, u32[]{:S(2)}, u32[]{:S(2)}) collective-permute-start(f32[128,1024]{1,0:T(8,128)} %pad_maximum_fusion.1), channel_id=1, source_target_pairs={{0,12},{4,0},{8,4},{12,8},{1,13},{5,1},{9,5},{13,9},{2,14},{6,2},{... | collective-permute-start | bytes 1572872 | tf_op jit(solution)/shard_map/ppermute | solution.py:365
  92.1 9.2 %all-to-all-done.1.parts = bf16[8,208,256]{2,1,0:T(8,128)(2,1)S(1)} async-done(((bf16[8,208,256]{2,1,0:T(8,128)(2,1)}), bf16[8,208,256]{2,1,0:T(8,128)(2,1)S(1)}, u32[]{:S(2)}, u32[]{:S(2)}) %all-to-all-start.1) | async-done | bytes 852000 | tf_op jit(solution)/shard_map/all_to_all | solution.py:369
  102.0 5.0 %all-to-all-start.2 = ((f32[32,8,128]{2,1,0:T(8,128)}), f32[32,8,128]{2,1,0:T(8,128)}, u32[]{:S(2)}, u32[]{:S(2)}) async-start(f32[32,8,128]{2,1,0:T(8,128)} %broadcast_in_dim.57), calls=%async_computation.2 | async-start | bytes 262144 | tf_op jit(solution)/shard_map/all_to_all | solution.py:369
  108.6 2.6 %collective-permute-start.17 = (bf16[32,1024]{1,0:T(8,128)(2,1)S(1)}, bf16[32,1024]{1,0:T(8,128)(2,1)S(1)}, u32[]{:S(2)}, u32[]{:S(2)}) collective-permute-start(bf16[32,1024]{1,0:T(8,128)(2,1)S(1)} %get-tuple-element.48), channel_id=1, source_target_pairs={{0,2},{1,3},{2,0},{3,1},{4,6},{5,7},{6,4},{7,5},{8,10},{9,11},{10,... | collective-permute-start | bytes 196616 | tf_op jit(solution)/shard_map/ppermute | solution.py:365
  111.2 1.9 %collective-permute-done.16.refs_1_ = bf16[32,1024]{1,0:T(8,128)(2,1)S(1)} collective-permute-done((bf16[32,1024]{1,0:T(8,128)(2,1)S(1)}, bf16[32,1024]{1,0:T(8,128)(2,1)S(1)}, u32[]{:S(2)}, u32[]{:S(2)}) %collective-permute-start.16) | collective-permute-done | bytes 65568 | tf_op jit(solution)/shard_map/ppermute | solution.py:365
  114.3 2.3 %collective-permute-done.18.refs_3_ = bf16[32,1024]{1,0:T(8,128)(2,1)S(1)} collective-permute-done((bf16[32,1024]{1,0:T(8,128)(2,1)S(1)}, bf16[32,1024]{1,0:T(8,128)(2,1)S(1)}, u32[]{:S(2)}, u32[]{:S(2)}) %collective-permute-start.18) | collective-permute-done | bytes 65568 | tf_op jit(solution)/shard_map/ppermute | solution.py:365
  (83 shorter events, 20.0 us)
Async XLA Ops:
  2.4 31.7 %all-to-all-start = ((bf16[8,192,256]{2,1,0:T(8,128)(2,1)}), bf16[8,192,256]{2,1,0:T(8,128)(2,1)S(1)}, u32[]{:S(2)}, u32[]{:S(2)}) async-start(bf16[8,192,256]{2,1,0:T(8,128)(2,1)} %broadcast_in_dim.48), calls=%async_computation | async-start | bytes 1572864 | tf_op jit(solution)/shard_map/all_to_all | solution.py:369
  12.4 9.8 %collective-permute-start = (bf16[144,1024]{1,0:T(8,128)(2,1)S(1)}, bf16[144,1024]{1,0:T(8,128)(2,1)S(1)}, u32[]{:S(2)}, u32[]{:S(2)}) collective-permute-start(bf16[144,1024]{1,0:T(8,128)(2,1)S(1)} %pad_maximum_fusion.2.refs_0_.refs_8_), channel_id=1, source_target_pairs={{0,4},{4,8},{8,12},{12,0},{1,5},{5,9},{9,13},{13,1},{2,6},{6,10},{... | collective-permute-start | bytes 884744 | tf_op jit(solution)/shard_map/ppermute | solution.py:365
  14.1 19.5 %collective-permute-start.1 = (bf16[144,1024]{1,0:T(8,128)(2,1)S(1)}, bf16[144,1024]{1,0:T(8,128)(2,1)S(1)}, u32[]{:S(2)}, u32[]{:S(2)}) collective-permute-start(bf16[144,1024]{1,0:T(8,128)(2,1)S(1)} %pad_maximum_fusion.2.refs_0_.refs_8_), channel_id=1, source_target_pairs={{0,12},{4,0},{8,4},{12,8},{1,13},{5,1},{9,5},{13,9},{2,14},{6,2},{... | collective-permute-start | bytes 884744 | tf_op jit(solution)/shard_map/ppermute | solution.py:365
  22.3 11.3 %collective-permute-start.2 = (bf16[144,1024]{1,0:T(8,128)(2,1)S(1)}, bf16[144,1024]{1,0:T(8,128)(2,1)S(1)}, u32[]{:S(2)}, u32[]{:S(2)}) collective-permute-start(bf16[144,1024]{1,0:T(8,128)(2,1)S(1)} %collective-permute-done.refs_2_.refs_10_), channel_id=1, source_target_pairs={{0,4},{4,8},{8,12},{12,0},{1,5},{5,9},{9,13},{13,1},{2,6},{6,10},{... | collective-permute-start | bytes 884744 | tf_op jit(solution)/shard_map/ppermute | solution.py:365
  22.7 7.2 %collective-permute-start.6 = (bf16[128,1024]{1,0:T(8,128)(2,1)S(1)}, bf16[128,1024]{1,0:T(8,128)(2,1)S(1)}, u32[]{:S(2)}, u32[]{:S(2)}) collective-permute-start(bf16[128,1024]{1,0:T(8,128)(2,1)S(1)} %fusion.refs_4_), channel_id=1, source_target_pairs={{0,12},{4,0},{8,4},{12,8},{1,13},{5,1},{9,5},{13,9},{2,14},{6,2},{... | collective-permute-start | bytes 786440 | tf_op jit(solution)/shard_map/ppermute | solution.py:365
  25.7 20.1 %collective-permute-start.7 = (bf16[128,1024]{1,0:T(8,128)(2,1)S(1)}, bf16[128,1024]{1,0:T(8,128)(2,1)S(1)}, u32[]{:S(2)}, u32[]{:S(2)}) collective-permute-start(bf16[128,1024]{1,0:T(8,128)(2,1)S(1)} %fusion.refs_4_), channel_id=1, source_target_pairs={{0,4},{4,8},{8,12},{12,0},{1,5},{5,9},{9,13},{13,1},{2,6},{6,10},{... | collective-permute-start | bytes 786440 | tf_op jit(solution)/shard_map/ppermute | solution.py:365
  29.9 16.0 %collective-permute-start.8 = (bf16[128,1024]{1,0:T(8,128)(2,1)S(1)}, bf16[128,1024]{1,0:T(8,128)(2,1)S(1)}, u32[]{:S(2)}, u32[]{:S(2)}) collective-permute-start(bf16[128,1024]{1,0:T(8,128)(2,1)S(1)} %collective-permute-done.6.refs_5_), channel_id=1, source_target_pairs={{0,12},{4,0},{8,4},{12,8},{1,13},{5,1},{9,5},{13,9},{2,14},{6,2},{... | collective-permute-start | bytes 786440 | tf_op jit(solution)/shard_map/ppermute | solution.py:365
  34.1 15.8 %copy-start.1 = (bf16[8,192,256]{2,1,0:T(8,128)(2,1)}, bf16[8,192,256]{2,1,0:T(8,128)(2,1)S(1)}, u32[]{:S(2)}) copy-start(bf16[8,192,256]{2,1,0:T(8,128)(2,1)S(1)} %all-to-all-done) | copy-start | bytes 2359300
  40.5 16.0 %copy-start.11 = (bf16[4,1024,128]{2,1,0:T(8,128)(2,1)}, bf16[4,1024,128]{2,1,0:T(8,128)(2,1)S(1)}, u32[]{:S(2)}) copy-start(bf16[4,1024,128]{2,1,0:T(8,128)(2,1)S(1)} %get-tuple-element.35.qh) | copy-start | bytes 3145732
  40.5 5.5 %collective-permute-start.5 = (f32[4,16,128]{2,1,0:T(8,128)S(1)}, f32[4,16,128]{2,1,0:T(8,128)S(1)}, u32[]{:S(2)}, u32[]{:S(2)}) collective-permute-start(f32[4,16,128]{2,1,0:T(8,128)S(1)} %get-tuple-element.38.refs_0_), channel_id=1, source_target_pairs={{0,8},{4,12},{8,0},{12,4},{1,9},{5,13},{9,1},{13,5},{2,10},{6,14},... | collective-permute-start | bytes 98312 | tf_op jit(solution)/shard_map/ppermute | solution.py:365
  43.8 3.9 %collective-permute-start.4 = (f32[4,16,128]{2,1,0:T(8,128)S(1)}, f32[4,16,128]{2,1,0:T(8,128)S(1)}, u32[]{:S(2)}, u32[]{:S(2)}) collective-permute-start(f32[4,16,128]{2,1,0:T(8,128)S(1)} %get-tuple-element.38.refs_0_), channel_id=1, source_target_pairs={{0,12},{4,0},{8,4},{12,8},{1,13},{5,1},{9,5},{13,9},{2,14},{6,2},{... | collective-permute-start | bytes 98312 | tf_op jit(solution)/shard_map/ppermute | solution.py:365
  44.8 5.1 %collective-permute-start.3 = (f32[4,16,128]{2,1,0:T(8,128)S(1)}, f32[4,16,128]{2,1,0:T(8,128)S(1)}, u32[]{:S(2)}, u32[]{:S(2)}) collective-permute-start(f32[4,16,128]{2,1,0:T(8,128)S(1)} %get-tuple-element.38.refs_0_), channel_id=1, source_target_pairs={{0,4},{4,8},{8,12},{12,0},{1,5},{5,9},{9,13},{13,1},{2,6},{6,10},{... | collective-permute-start | bytes 98312 | tf_op jit(solution)/shard_map/ppermute | solution.py:365
  56.5 5.3 %collective-permute-start.11 = (f32[4,8,128]{2,1,0:T(8,128)S(1)}, f32[4,8,128]{2,1,0:T(8,128)S(1)}, u32[]{:S(2)}, u32[]{:S(2)}) collective-permute-start(f32[4,8,128]{2,1,0:T(8,128)S(1)} %get-tuple-element.41.refs_0_), channel_id=1, source_target_pairs={{0,8},{4,12},{8,0},{12,4},{1,9},{5,13},{9,1},{13,5},{2,10},{6,14},... | collective-permute-start | bytes 49160 | tf_op jit(solution)/shard_map/ppermute | solution.py:365
  57.1 4.8 %collective-permute-start.10 = (f32[4,8,128]{2,1,0:T(8,128)S(1)}, f32[4,8,128]{2,1,0:T(8,128)S(1)}, u32[]{:S(2)}, u32[]{:S(2)}) collective-permute-start(f32[4,8,128]{2,1,0:T(8,128)S(1)} %get-tuple-element.41.refs_0_), channel_id=1, source_target_pairs={{0,12},{4,0},{8,4},{12,8},{1,13},{5,1},{9,5},{13,9},{2,14},{6,2},{... | collective-permute-start | bytes 49160 | tf_op jit(solution)/shard_map/ppermute | solution.py:365
  59.0 5.0 %collective-permute-start.9 = (f32[4,8,128]{2,1,0:T(8,128)S(1)}, f32[4,8,128]{2,1,0:T(8,128)S(1)}, u32[]{:S(2)}, u32[]{:S(2)}) collective-permute-start(f32[4,8,128]{2,1,0:T(8,128)S(1)} %get-tuple-element.41.refs_0_), channel_id=1, source_target_pairs={{0,4},{4,8},{8,12},{12,0},{1,5},{5,9},{9,13},{13,1},{2,6},{6,10},{... | collective-permute-start | bytes 49160 | tf_op jit(solution)/shard_map/ppermute | solution.py:365
  75.8 25.5 %all-to-all-start.1 = ((bf16[8,208,256]{2,1,0:T(8,128)(2,1)}), bf16[8,208,256]{2,1,0:T(8,128)(2,1)S(1)}, u32[]{:S(2)}, u32[]{:S(2)}) async-start(bf16[8,208,256]{2,1,0:T(8,128)(2,1)} %get-tuple-element.52), calls=%async_computation.1 | async-start | bytes 1703936 | tf_op jit(solution)/shard_map/all_to_all | solution.py:369
  79.7 8.0 %collective-permute-start.12 = (f32[128,512]{1,0:T(8,128)S(1)}, f32[128,512]{1,0:T(8,128)S(1)}, u32[]{:S(2)}, u32[]{:S(2)}) collective-permute-start(f32[128,512]{1,0:T(8,128)S(1)} %get-tuple-element.58), channel_id=1, source_target_pairs={{0,4},{4,8},{8,12},{12,0},{1,5},{5,9},{9,13},{13,1},{2,6},{6,10},{... | collective-permute-start | bytes 786440 | tf_op jit(solution)/shard_map/ppermute | solution.py:365
  79.8 8.1 %collective-permute-start.14 = (f32[128,512]{1,0:T(8,128)S(1)}, f32[128,512]{1,0:T(8,128)S(1)}, u32[]{:S(2)}, u32[]{:S(2)}) collective-permute-start(f32[128,512]{1,0:T(8,128)S(1)} %get-tuple-element.57), channel_id=1, source_target_pairs={{0,12},{4,0},{8,4},{12,8},{1,13},{5,1},{9,5},{13,9},{2,14},{6,2},{... | collective-permute-start | bytes 786440 | tf_op jit(solution)/shard_map/ppermute | solution.py:365
  87.9 19.1 %collective-permute-start.13 = (f32[128,1024]{1,0:T(8,128)S(1)}, f32[128,1024]{1,0:T(8,128)S(1)}, u32[]{:S(2)}, u32[]{:S(2)}) collective-permute-start(f32[128,1024]{1,0:T(8,128)S(1)} %pad_maximum_fusion), channel_id=1, source_target_pairs={{0,4},{4,8},{8,12},{12,0},{1,5},{5,9},{9,13},{13,1},{2,6},{6,10},{... | collective-permute-start | bytes 1572872 | tf_op jit(solution)/shard_map/ppermute | solution.py:365
  89.7 17.3 %collective-permute-start.15 = (f32[128,1024]{1,0:T(8,128)}, f32[128,1024]{1,0:T(8,128)S(1)}, u32[]{:S(2)}, u32[]{:S(2)}) collective-permute-start(f32[128,1024]{1,0:T(8,128)} %pad_maximum_fusion.1), channel_id=1, source_target_pairs={{0,12},{4,0},{8,4},{12,8},{1,13},{5,1},{9,5},{13,9},{2,14},{6,2},{... | collective-permute-start | bytes 1572872 | tf_op jit(solution)/shard_map/ppermute | solution.py:365
  102.0 16.9 %all-to-all-start.2 = ((f32[32,8,128]{2,1,0:T(8,128)}), f32[32,8,128]{2,1,0:T(8,128)}, u32[]{:S(2)}, u32[]{:S(2)}) async-start(f32[32,8,128]{2,1,0:T(8,128)} %broadcast_in_dim.57), calls=%async_computation.2 | async-start | bytes 262144 | tf_op jit(solution)/shard_map/all_to_all | solution.py:369
  108.2 4.9 %collective-permute-start.16 = (bf16[32,1024]{1,0:T(8,128)(2,1)S(1)}, bf16[32,1024]{1,0:T(8,128)(2,1)S(1)}, u32[]{:S(2)}, u32[]{:S(2)}) collective-permute-start(bf16[32,1024]{1,0:T(8,128)(2,1)S(1)} %get-tuple-element.47), channel_id=1, source_target_pairs={{0,1},{1,2},{2,3},{3,0},{4,5},{5,6},{6,7},{7,4},{8,9},{9,10},{10,1... | collective-permute-start | bytes 196616 | tf_op jit(solution)/shard_map/ppermute | solution.py:365
  108.6 5.8 %collective-permute-start.17 = (bf16[32,1024]{1,0:T(8,128)(2,1)S(1)}, bf16[32,1024]{1,0:T(8,128)(2,1)S(1)}, u32[]{:S(2)}, u32[]{:S(2)}) collective-permute-start(bf16[32,1024]{1,0:T(8,128)(2,1)S(1)} %get-tuple-element.48), channel_id=1, source_target_pairs={{0,2},{1,3},{2,0},{3,1},{4,6},{5,7},{6,4},{7,5},{8,10},{9,11},{10,... | collective-permute-start | bytes 196616 | tf_op jit(solution)/shard_map/ppermute | solution.py:365
  111.2 5.5 %collective-permute-start.18 = (bf16[32,1024]{1,0:T(8,128)(2,1)S(1)}, bf16[32,1024]{1,0:T(8,128)(2,1)S(1)}, u32[]{:S(2)}, u32[]{:S(2)}) collective-permute-start(bf16[32,1024]{1,0:T(8,128)(2,1)S(1)} %get-tuple-element.49), channel_id=1, source_target_pairs={{0,3},{1,0},{2,1},{3,2},{4,7},{5,4},{6,5},{7,6},{8,11},{9,8},{10,9... | collective-permute-start | bytes 196616 | tf_op jit(solution)/shard_map/ppermute | solution.py:365
  (15 other events, 86.5 us)

commit v3 on v2

--- a/solution.py
+++ b/solution.py
@@ -91,8 +91,8 @@
 def terms_of(rest):
     terms = []
     for _ in range(3):
-        terms.append(rest.astype(BF16))
-        rest = rest - terms[-1].astype(F32)
+        terms.append(rest.astype(BF16).astype(F32))
+        rest = rest - terms[-1]
     return terms
 
 
@@ -251,10 +251,10 @@
     u = unit(kv[:, :HEAD].astype(F32))
     gain_k = gain_k + jnp.sum(scaled * u, axis=0, keepdims=True)
     terms = terms_of(jnp.concatenate([gain_q, gain_k, jnp.zeros((6, HEAD), F32)], axis=0))
-    terms.append(jnp.zeros((8, HEAD), BF16))
+    terms.append(jnp.zeros((8, HEAD), F32))
     rows = jnp.concatenate(
         [jnp.concatenate(terms[:2], axis=0), jnp.concatenate(terms[2:], axis=0)], axis=1
-    )
+    ).astype(BF16)
     for c in range(Z):
         out[c, ROWS:, :] = rows
 

time: 121 us -> 121 us (level)
  no operation moved by 1% of the time
where the time goes in v3:
time: 121 us; the launch traced here: 120 us
  starting transfers between devices  44.4 us (37%)
  waiting for transfers between devices  38.3 us (32%)
  Pallas kernels  25.4 us (21%)
  local copies, waits for them, and re-layouts  6.39 us (5%)
  other arithmetic  3.07 us (3%)
  between operations  2.82 us (2%)
    ppermute x19, waiting for transfers between devices, shift(): return lax.ppermute(x, axis, [(i, (i + step) % size) for i in range(size)])  28.5 us
    ppermute x19, starting transfers between devices, shift(): return lax.ppermute(x, axis, [(i, (i + step) % size) for i in range(size)])  27 us
    pallas_call x6, Pallas kernels, call(): pl.pallas_call(kernel, out_shape=out_shape, in_specs=specs, out_specs=jax...  25.4 us
    all_to_all x3, starting transfers between devices, to_all(): return lax.all_to_all(x, axis, 0, 0, tiled=False)  17.5 us
    all_to_all x3, waiting for transfers between devices, to_all(): return lax.all_to_all(x, axis, 0, 0, tiled=False)  9.81 us
    unnamed x34, local copies, waits for them, and re-layouts  4.21 us
  transfers between devices with their start and end apart: 22, of which 13 were waited for; matrix products, arithmetic and copies ran while one was open for 2% of the time, Pallas kernels for 7%

profile of v3, /device:TPU:6, one launch (start us, length us, event | category | flops | bytes accessed | tf_op | source)
XLA Modules:
  0.0 120.4 jit_solution(5923985133587395297)
XLA Ops:
  2.4 8.6 %all-to-all-start = ((bf16[8,192,256]{2,1,0:T(8,128)(2,1)}), bf16[8,192,256]{2,1,0:T(8,128)(2,1)S(1)}, u32[]{:S(2)}, u32[]{:S(2)}) async-start(bf16[8,192,256]{2,1,0:T(8,128)(2,1)} %broadcast_in_dim.48), calls=%async_computation | async-start | bytes 1572864 | tf_op jit(solution)/shard_map/all_to_all | solution.py:369
  14.1 1.7 %collective-permute-start.1 = (bf16[144,1024]{1,0:T(8,128)(2,1)S(1)}, bf16[144,1024]{1,0:T(8,128)(2,1)S(1)}, u32[]{:S(2)}, u32[]{:S(2)}) collective-permute-start(bf16[144,1024]{1,0:T(8,128)(2,1)S(1)} %pad_maximum_fusion.2.refs_0_.refs_8_), channel_id=1, source_target_pairs={{0,12},{4,0},{8,4},{12,8},{1,13},{5,1},{9,5},{13,9},{2,14},{6,2},{... | collective-permute-start | bytes 884744 | tf_op jit(solution)/shard_map/ppermute | solution.py:365
  17.1 5.2 %collective-permute-done.refs_2_.refs_10_ = bf16[144,1024]{1,0:T(8,128)(2,1)S(1)} collective-permute-done((bf16[144,1024]{1,0:T(8,128)(2,1)S(1)}, bf16[144,1024]{1,0:T(8,128)(2,1)S(1)}, u32[]{:S(2)}, u32[]{:S(2)}) %collective-permute-start) | collective-permute-done | bytes 294944 | tf_op jit(solution)/shard_map/ppermute | solution.py:365
  22.7 3.0 %collective-permute-start.6 = (bf16[128,1024]{1,0:T(8,128)(2,1)S(1)}, bf16[128,1024]{1,0:T(8,128)(2,1)S(1)}, u32[]{:S(2)}, u32[]{:S(2)}) collective-permute-start(bf16[128,1024]{1,0:T(8,128)(2,1)S(1)} %fusion.refs_4_), channel_id=1, source_target_pairs={{0,12},{4,0},{8,4},{12,8},{1,13},{5,1},{9,5},{13,9},{2,14},{6,2},{... | collective-permute-start | bytes 786440 | tf_op jit(solution)/shard_map/ppermute | solution.py:365
  25.8 4.1 %collective-permute-done.6.refs_5_ = bf16[128,1024]{1,0:T(8,128)(2,1)S(1)} collective-permute-done((bf16[128,1024]{1,0:T(8,128)(2,1)S(1)}, bf16[128,1024]{1,0:T(8,128)(2,1)S(1)}, u32[]{:S(2)}, u32[]{:S(2)}) %collective-permute-start.6) | collective-permute-done | bytes 262176 | tf_op jit(solution)/shard_map/ppermute | solution.py:365
  29.9 3.7 %collective-permute-start.8 = (bf16[128,1024]{1,0:T(8,128)(2,1)S(1)}, bf16[128,1024]{1,0:T(8,128)(2,1)S(1)}, u32[]{:S(2)}, u32[]{:S(2)}) collective-permute-start(bf16[128,1024]{1,0:T(8,128)(2,1)S(1)} %collective-permute-done.6.refs_5_), channel_id=1, source_target_pairs={{0,12},{4,0},{8,4},{12,8},{1,13},{5,1},{9,5},{13,9},{2,14},{6,2},{... | collective-permute-start | bytes 786440 | tf_op jit(solution)/shard_map/ppermute | solution.py:365
  34.9 5.6 %shard_map.171 = (bf16[4,1024,128]{2,1,0:T(8,128)(2,1)S(1)}, bf16[1536,128]{1,0:T(8,128)(2,1)S(1)}, bf16[128,128]{1,0:T(8,128)(2,1)S(1)}, f32[4,16,128]{2,1,0:T(8,128)S(1)}) custom-call(s32[3]{0:T(128)S(1)} %pad_add_fusion.pos, s32[4,128]{1,0:T(4,128)S(1)} %maximum_convert_fusion.info, f32[1,128]{1,0:T(1,128)S(1)} %bitcast.40, f32[1,128]{1,0:T(1,128)S(1)} %bitcast.42, ...), custom_call_target="tpu_custom_call" | custom-call | flops 1610612736 | bytes 4194304 | tf_op jit(solution)/shard_map/pallas_call | solution.py:289
  40.5 3.3 %collective-permute-start.5 = (f32[4,16,128]{2,1,0:T(8,128)S(1)}, f32[4,16,128]{2,1,0:T(8,128)S(1)}, u32[]{:S(2)}, u32[]{:S(2)}) collective-permute-start(f32[4,16,128]{2,1,0:T(8,128)S(1)} %get-tuple-element.38.refs_0_), channel_id=1, source_target_pairs={{0,8},{4,12},{8,0},{12,4},{1,9},{5,13},{9,1},{13,5},{2,10},{6,14},... | collective-permute-start | bytes 98312 | tf_op jit(solution)/shard_map/ppermute | solution.py:365
  46.0 1.7 %collective-permute-done.4.refs_2_ = f32[4,16,128]{2,1,0:T(8,128)S(1)} collective-permute-done((f32[4,16,128]{2,1,0:T(8,128)S(1)}, f32[4,16,128]{2,1,0:T(8,128)S(1)}, u32[]{:S(2)}, u32[]{:S(2)}) %collective-permute-start.4) | collective-permute-done | bytes 32800 | tf_op jit(solution)/shard_map/ppermute | solution.py:365
  47.7 2.3 %collective-permute-done.3.refs_1_ = f32[4,16,128]{2,1,0:T(8,128)S(1)} collective-permute-done((f32[4,16,128]{2,1,0:T(8,128)S(1)}, f32[4,16,128]{2,1,0:T(8,128)S(1)}, u32[]{:S(2)}, u32[]{:S(2)}) %collective-permute-start.3) | collective-permute-done | bytes 32800 | tf_op jit(solution)/shard_map/ppermute | solution.py:365
  50.0 6.5 %shard_map.172 = (bf16[1536,128]{1,0:T(8,128)(2,1)S(1)}, f32[128,128]{1,0:T(8,128)}, f32[4,8,128]{2,1,0:T(8,128)S(1)}, f32[4,8,128]{2,1,0:T(8,128)S(1)}) custom-call(s32[3]{0:T(128)S(1)} %pad_add_fusion.pos, s32[4,128]{1,0:T(4,128)S(1)} %maximum_convert_fusion.info, bf16[4,1024,128]{2,1,0:T(8,128)(2,1)S(1)} %get-tuple-element.35.qh, ...), custom_call_target="tpu_custom_call" | custom-call | flops 3221225472 | bytes 4194304 | tf_op jit(solution)/shard_map/pallas_call | solution.py:289
  57.1 1.9 %collective-permute-start.10 = (f32[4,8,128]{2,1,0:T(8,128)S(1)}, f32[4,8,128]{2,1,0:T(8,128)S(1)}, u32[]{:S(2)}, u32[]{:S(2)}) collective-permute-start(f32[4,8,128]{2,1,0:T(8,128)S(1)} %get-tuple-element.41.refs_0_), channel_id=1, source_target_pairs={{0,12},{4,0},{8,4},{12,8},{1,13},{5,1},{9,5},{13,9},{2,14},{6,2},{... | collective-permute-start | bytes 49160 | tf_op jit(solution)/shard_map/ppermute | solution.py:365
  59.1 2.7 %collective-permute-done.11.refs_3_ = f32[4,8,128]{2,1,0:T(8,128)S(1)} collective-permute-done((f32[4,8,128]{2,1,0:T(8,128)S(1)}, f32[4,8,128]{2,1,0:T(8,128)S(1)}, u32[]{:S(2)}, u32[]{:S(2)}) %collective-permute-start.11) | collective-permute-done | bytes 16416 | tf_op jit(solution)/shard_map/ppermute | solution.py:365
  61.8 2.1 %collective-permute-done.9.refs_1_ = f32[4,8,128]{2,1,0:T(8,128)S(1)} collective-permute-done((f32[4,8,128]{2,1,0:T(8,128)S(1)}, f32[4,8,128]{2,1,0:T(8,128)S(1)}, u32[]{:S(2)}, u32[]{:S(2)}) %collective-permute-start.9) | collective-permute-done | bytes 16416 | tf_op jit(solution)/shard_map/ppermute | solution.py:365
  65.9 9.9 %shard_map.173 = (f32[128,1024]{1,0:T(8,128)S(1)}, f32[128,1024]{1,0:T(8,128)}, f32[128,1024]{1,0:T(8,128)}, f32[2,128,512]{2,1,0:T(8,128)}, bf16[8,208,256]{2,1,0:T(8,128)(2,1)}, /*index=5*/f32[128,128]{1,0:T(8,128)}) custom-call(s32[3]{0:T(128)S(1)} %pad_add_fusion.pos, s32[4,128]{1,0:T(4,128)S(1)} %maximum_convert_fusion.info, ...), custom_call_target="tpu_custom_call" | custom-call | flops 4026531840 | bytes 4194304 | tf_op jit(solution)/shard_map/pallas_call | solution.py:289
  75.8 3.9 %all-to-all-start.1 = ((bf16[8,208,256]{2,1,0:T(8,128)(2,1)}), bf16[8,208,256]{2,1,0:T(8,128)(2,1)S(1)}, u32[]{:S(2)}, u32[]{:S(2)}) async-start(bf16[8,208,256]{2,1,0:T(8,128)(2,1)} %get-tuple-element.52), calls=%async_computation.1 | async-start | bytes 1703936 | tf_op jit(solution)/shard_map/all_to_all | solution.py:369
  79.8 3.2 %collective-permute-start.14 = (f32[128,512]{1,0:T(8,128)S(1)}, f32[128,512]{1,0:T(8,128)S(1)}, u32[]{:S(2)}, u32[]{:S(2)}) collective-permute-start(f32[128,512]{1,0:T(8,128)S(1)} %get-tuple-element.57), channel_id=1, source_target_pairs={{0,12},{4,0},{8,4},{12,8},{1,13},{5,1},{9,5},{13,9},{2,14},{6,2},{... | collective-permute-start | bytes 786440 | tf_op jit(solution)/shard_map/ppermute | solution.py:365
  83.0 4.7 %collective-permute-done.12 = f32[128,512]{1,0:T(8,128)S(1)} collective-permute-done((f32[128,512]{1,0:T(8,128)S(1)}, f32[128,512]{1,0:T(8,128)S(1)}, u32[]{:S(2)}, u32[]{:S(2)}) %collective-permute-start.12) | collective-permute-done | bytes 262176 | tf_op jit(solution)/shard_map/ppermute | solution.py:365
  89.7 2.3 %collective-permute-start.15 = (f32[128,1024]{1,0:T(8,128)}, f32[128,1024]{1,0:T(8,128)S(1)}, u32[]{:S(2)}, u32[]{:S(2)}) collective-permute-start(f32[128,1024]{1,0:T(8,128)} %pad_maximum_fusion.1), channel_id=1, source_target_pairs={{0,12},{4,0},{8,4},{12,8},{1,13},{5,1},{9,5},{13,9},{2,14},{6,2},{... | collective-permute-start | bytes 1572872 | tf_op jit(solution)/shard_map/ppermute | solution.py:365
  92.1 9.2 %all-to-all-done.1.parts = bf16[8,208,256]{2,1,0:T(8,128)(2,1)S(1)} async-done(((bf16[8,208,256]{2,1,0:T(8,128)(2,1)}), bf16[8,208,256]{2,1,0:T(8,128)(2,1)S(1)}, u32[]{:S(2)}, u32[]{:S(2)}) %all-to-all-start.1) | async-done | bytes 852000 | tf_op jit(solution)/shard_map/all_to_all | solution.py:369
  102.0 5.0 %all-to-all-start.2 = ((f32[32,8,128]{2,1,0:T(8,128)}), f32[32,8,128]{2,1,0:T(8,128)}, u32[]{:S(2)}, u32[]{:S(2)}) async-start(f32[32,8,128]{2,1,0:T(8,128)} %broadcast_in_dim.57), calls=%async_computation.2 | async-start | bytes 262144 | tf_op jit(solution)/shard_map/all_to_all | solution.py:369
  108.6 2.6 %collective-permute-start.17 = (bf16[32,1024]{1,0:T(8,128)(2,1)S(1)}, bf16[32,1024]{1,0:T(8,128)(2,1)S(1)}, u32[]{:S(2)}, u32[]{:S(2)}) collective-permute-start(bf16[32,1024]{1,0:T(8,128)(2,1)S(1)} %get-tuple-element.48), channel_id=1, source_target_pairs={{0,2},{1,3},{2,0},{3,1},{4,6},{5,7},{6,4},{7,5},{8,10},{9,11},{10,... | collective-permute-start | bytes 196616 | tf_op jit(solution)/shard_map/ppermute | solution.py:365
  111.2 1.9 %collective-permute-done.16.refs_1_ = bf16[32,1024]{1,0:T(8,128)(2,1)S(1)} collective-permute-done((bf16[32,1024]{1,0:T(8,128)(2,1)S(1)}, bf16[32,1024]{1,0:T(8,128)(2,1)S(1)}, u32[]{:S(2)}, u32[]{:S(2)}) %collective-permute-start.16) | collective-permute-done | bytes 65568 | tf_op jit(solution)/shard_map/ppermute | solution.py:365
  114.3 2.3 %collective-permute-done.18.refs_3_ = bf16[32,1024]{1,0:T(8,128)(2,1)S(1)} collective-permute-done((bf16[32,1024]{1,0:T(8,128)(2,1)S(1)}, bf16[32,1024]{1,0:T(8,128)(2,1)S(1)}, u32[]{:S(2)}, u32[]{:S(2)}) %collective-permute-start.18) | collective-permute-done | bytes 65568 | tf_op jit(solution)/shard_map/ppermute | solution.py:365
  (83 shorter events, 20.0 us)
Async XLA Ops:
  2.4 31.7 %all-to-all-start = ((bf16[8,192,256]{2,1,0:T(8,128)(2,1)}), bf16[8,192,256]{2,1,0:T(8,128)(2,1)S(1)}, u32[]{:S(2)}, u32[]{:S(2)}) async-start(bf16[8,192,256]{2,1,0:T(8,128)(2,1)} %broadcast_in_dim.48), calls=%async_computation | async-start | bytes 1572864 | tf_op jit(solution)/shard_map/all_to_all | solution.py:369
  12.4 9.8 %collective-permute-start = (bf16[144,1024]{1,0:T(8,128)(2,1)S(1)}, bf16[144,1024]{1,0:T(8,128)(2,1)S(1)}, u32[]{:S(2)}, u32[]{:S(2)}) collective-permute-start(bf16[144,1024]{1,0:T(8,128)(2,1)S(1)} %pad_maximum_fusion.2.refs_0_.refs_8_), channel_id=1, source_target_pairs={{0,4},{4,8},{8,12},{12,0},{1,5},{5,9},{9,13},{13,1},{2,6},{6,10},{... | collective-permute-start | bytes 884744 | tf_op jit(solution)/shard_map/ppermute | solution.py:365
  14.1 19.5 %collective-permute-start.1 = (bf16[144,1024]{1,0:T(8,128)(2,1)S(1)}, bf16[144,1024]{1,0:T(8,128)(2,1)S(1)}, u32[]{:S(2)}, u32[]{:S(2)}) collective-permute-start(bf16[144,1024]{1,0:T(8,128)(2,1)S(1)} %pad_maximum_fusion.2.refs_0_.refs_8_), channel_id=1, source_target_pairs={{0,12},{4,0},{8,4},{12,8},{1,13},{5,1},{9,5},{13,9},{2,14},{6,2},{... | collective-permute-start | bytes 884744 | tf_op jit(solution)/shard_map/ppermute | solution.py:365
  22.3 11.3 %collective-permute-start.2 = (bf16[144,1024]{1,0:T(8,128)(2,1)S(1)}, bf16[144,1024]{1,0:T(8,128)(2,1)S(1)}, u32[]{:S(2)}, u32[]{:S(2)}) collective-permute-start(bf16[144,1024]{1,0:T(8,128)(2,1)S(1)} %collective-permute-done.refs_2_.refs_10_), channel_id=1, source_target_pairs={{0,4},{4,8},{8,12},{12,0},{1,5},{5,9},{9,13},{13,1},{2,6},{6,10},{... | collective-permute-start | bytes 884744 | tf_op jit(solution)/shard_map/ppermute | solution.py:365
  22.7 7.2 %collective-permute-start.6 = (bf16[128,1024]{1,0:T(8,128)(2,1)S(1)}, bf16[128,1024]{1,0:T(8,128)(2,1)S(1)}, u32[]{:S(2)}, u32[]{:S(2)}) collective-permute-start(bf16[128,1024]{1,0:T(8,128)(2,1)S(1)} %fusion.refs_4_), channel_id=1, source_target_pairs={{0,12},{4,0},{8,4},{12,8},{1,13},{5,1},{9,5},{13,9},{2,14},{6,2},{... | collective-permute-start | bytes 786440 | tf_op jit(solution)/shard_map/ppermute | solution.py:365
  25.7 20.1 %collective-permute-start.7 = (bf16[128,1024]{1,0:T(8,128)(2,1)S(1)}, bf16[128,1024]{1,0:T(8,128)(2,1)S(1)}, u32[]{:S(2)}, u32[]{:S(2)}) collective-permute-start(bf16[128,1024]{1,0:T(8,128)(2,1)S(1)} %fusion.refs_4_), channel_id=1, source_target_pairs={{0,4},{4,8},{8,12},{12,0},{1,5},{5,9},{9,13},{13,1},{2,6},{6,10},{... | collective-permute-start | bytes 786440 | tf_op jit(solution)/shard_map/ppermute | solution.py:365
  29.9 16.0 %collective-permute-start.8 = (bf16[128,1024]{1,0:T(8,128)(2,1)S(1)}, bf16[128,1024]{1,0:T(8,128)(2,1)S(1)}, u32[]{:S(2)}, u32[]{:S(2)}) collective-permute-start(bf16[128,1024]{1,0:T(8,128)(2,1)S(1)} %collective-permute-done.6.refs_5_), channel_id=1, source_target_pairs={{0,12},{4,0},{8,4},{12,8},{1,13},{5,1},{9,5},{13,9},{2,14},{6,2},{... | collective-permute-start | bytes 786440 | tf_op jit(solution)/shard_map/ppermute | solution.py:365
  34.1 15.8 %copy-start.1 = (bf16[8,192,256]{2,1,0:T(8,128)(2,1)}, bf16[8,192,256]{2,1,0:T(8,128)(2,1)S(1)}, u32[]{:S(2)}) copy-start(bf16[8,192,256]{2,1,0:T(8,128)(2,1)S(1)} %all-to-all-done) | copy-start | bytes 2359300
  40.5 16.0 %copy-start.11 = (bf16[4,1024,128]{2,1,0:T(8,128)(2,1)}, bf16[4,1024,128]{2,1,0:T(8,128)(2,1)S(1)}, u32[]{:S(2)}) copy-start(bf16[4,1024,128]{2,1,0:T(8,128)(2,1)S(1)} %get-tuple-element.35.qh) | copy-start | bytes 3145732
  40.5 5.5 %collective-permute-start.5 = (f32[4,16,128]{2,1,0:T(8,128)S(1)}, f32[4,16,128]{2,1,0:T(8,128)S(1)}, u32[]{:S(2)}, u32[]{:S(2)}) collective-permute-start(f32[4,16,128]{2,1,0:T(8,128)S(1)} %get-tuple-element.38.refs_0_), channel_id=1, source_target_pairs={{0,8},{4,12},{8,0},{12,4},{1,9},{5,13},{9,1},{13,5},{2,10},{6,14},... | collective-permute-start | bytes 98312 | tf_op jit(solution)/shard_map/ppermute | solution.py:365
  43.8 3.9 %collective-permute-start.4 = (f32[4,16,128]{2,1,0:T(8,128)S(1)}, f32[4,16,128]{2,1,0:T(8,128)S(1)}, u32[]{:S(2)}, u32[]{:S(2)}) collective-permute-start(f32[4,16,128]{2,1,0:T(8,128)S(1)} %get-tuple-element.38.refs_0_), channel_id=1, source_target_pairs={{0,12},{4,0},{8,4},{12,8},{1,13},{5,1},{9,5},{13,9},{2,14},{6,2},{... | collective-permute-start | bytes 98312 | tf_op jit(solution)/shard_map/ppermute | solution.py:365
  44.8 5.1 %collective-permute-start.3 = (f32[4,16,128]{2,1,0:T(8,128)S(1)}, f32[4,16,128]{2,1,0:T(8,128)S(1)}, u32[]{:S(2)}, u32[]{:S(2)}) collective-permute-start(f32[4,16,128]{2,1,0:T(8,128)S(1)} %get-tuple-element.38.refs_0_), channel_id=1, source_target_pairs={{0,4},{4,8},{8,12},{12,0},{1,5},{5,9},{9,13},{13,1},{2,6},{6,10},{... | collective-permute-start | bytes 98312 | tf_op jit(solution)/shard_map/ppermute | solution.py:365
  56.5 5.3 %collective-permute-start.11 = (f32[4,8,128]{2,1,0:T(8,128)S(1)}, f32[4,8,128]{2,1,0:T(8,128)S(1)}, u32[]{:S(2)}, u32[]{:S(2)}) collective-permute-start(f32[4,8,128]{2,1,0:T(8,128)S(1)} %get-tuple-element.41.refs_0_), channel_id=1, source_target_pairs={{0,8},{4,12},{8,0},{12,4},{1,9},{5,13},{9,1},{13,5},{2,10},{6,14},... | collective-permute-start | bytes 49160 | tf_op jit(solution)/shard_map/ppermute | solution.py:365
  57.1 4.8 %collective-permute-start.10 = (f32[4,8,128]{2,1,0:T(8,128)S(1)}, f32[4,8,128]{2,1,0:T(8,128)S(1)}, u32[]{:S(2)}, u32[]{:S(2)}) collective-permute-start(f32[4,8,128]{2,1,0:T(8,128)S(1)} %get-tuple-element.41.refs_0_), channel_id=1, source_target_pairs={{0,12},{4,0},{8,4},{12,8},{1,13},{5,1},{9,5},{13,9},{2,14},{6,2},{... | collective-permute-start | bytes 49160 | tf_op jit(solution)/shard_map/ppermute | solution.py:365
  59.0 5.0 %collective-permute-start.9 = (f32[4,8,128]{2,1,0:T(8,128)S(1)}, f32[4,8,128]{2,1,0:T(8,128)S(1)}, u32[]{:S(2)}, u32[]{:S(2)}) collective-permute-start(f32[4,8,128]{2,1,0:T(8,128)S(1)} %get-tuple-element.41.refs_0_), channel_id=1, source_target_pairs={{0,4},{4,8},{8,12},{12,0},{1,5},{5,9},{9,13},{13,1},{2,6},{6,10},{... | collective-permute-start | bytes 49160 | tf_op jit(solution)/shard_map/ppermute | solution.py:365
  75.8 25.5 %all-to-all-start.1 = ((bf16[8,208,256]{2,1,0:T(8,128)(2,1)}), bf16[8,208,256]{2,1,0:T(8,128)(2,1)S(1)}, u32[]{:S(2)}, u32[]{:S(2)}) async-start(bf16[8,208,256]{2,1,0:T(8,128)(2,1)} %get-tuple-element.52), calls=%async_computation.1 | async-start | bytes 1703936 | tf_op jit(solution)/shard_map/all_to_all | solution.py:369
  79.7 8.0 %collective-permute-start.12 = (f32[128,512]{1,0:T(8,128)S(1)}, f32[128,512]{1,0:T(8,128)S(1)}, u32[]{:S(2)}, u32[]{:S(2)}) collective-permute-start(f32[128,512]{1,0:T(8,128)S(1)} %get-tuple-element.58), channel_id=1, source_target_pairs={{0,4},{4,8},{8,12},{12,0},{1,5},{5,9},{9,13},{13,1},{2,6},{6,10},{... | collective-permute-start | bytes 786440 | tf_op jit(solution)/shard_map/ppermute | solution.py:365
  79.8 8.1 %collective-permute-start.14 = (f32[128,512]{1,0:T(8,128)S(1)}, f32[128,512]{1,0:T(8,128)S(1)}, u32[]{:S(2)}, u32[]{:S(2)}) collective-permute-start(f32[128,512]{1,0:T(8,128)S(1)} %get-tuple-element.57), channel_id=1, source_target_pairs={{0,12},{4,0},{8,4},{12,8},{1,13},{5,1},{9,5},{13,9},{2,14},{6,2},{... | collective-permute-start | bytes 786440 | tf_op jit(solution)/shard_map/ppermute | solution.py:365
  87.9 19.1 %collective-permute-start.13 = (f32[128,1024]{1,0:T(8,128)S(1)}, f32[128,1024]{1,0:T(8,128)S(1)}, u32[]{:S(2)}, u32[]{:S(2)}) collective-permute-start(f32[128,1024]{1,0:T(8,128)S(1)} %pad_maximum_fusion), channel_id=1, source_target_pairs={{0,4},{4,8},{8,12},{12,0},{1,5},{5,9},{9,13},{13,1},{2,6},{6,10},{... | collective-permute-start | bytes 1572872 | tf_op jit(solution)/shard_map/ppermute | solution.py:365
  89.7 17.3 %collective-permute-start.15 = (f32[128,1024]{1,0:T(8,128)}, f32[128,1024]{1,0:T(8,128)S(1)}, u32[]{:S(2)}, u32[]{:S(2)}) collective-permute-start(f32[128,1024]{1,0:T(8,128)} %pad_maximum_fusion.1), channel_id=1, source_target_pairs={{0,12},{4,0},{8,4},{12,8},{1,13},{5,1},{9,5},{13,9},{2,14},{6,2},{... | collective-permute-start | bytes 1572872 | tf_op jit(solution)/shard_map/ppermute | solution.py:365
  102.0 16.9 %all-to-all-start.2 = ((f32[32,8,128]{2,1,0:T(8,128)}), f32[32,8,128]{2,1,0:T(8,128)}, u32[]{:S(2)}, u32[]{:S(2)}) async-start(f32[32,8,128]{2,1,0:T(8,128)} %broadcast_in_dim.57), calls=%async_computation.2 | async-start | bytes 262144 | tf_op jit(solution)/shard_map/all_to_all | solution.py:369
  108.2 4.9 %collective-permute-start.16 = (bf16[32,1024]{1,0:T(8,128)(2,1)S(1)}, bf16[32,1024]{1,0:T(8,128)(2,1)S(1)}, u32[]{:S(2)}, u32[]{:S(2)}) collective-permute-start(bf16[32,1024]{1,0:T(8,128)(2,1)S(1)} %get-tuple-element.47), channel_id=1, source_target_pairs={{0,1},{1,2},{2,3},{3,0},{4,5},{5,6},{6,7},{7,4},{8,9},{9,10},{10,1... | collective-permute-start | bytes 196616 | tf_op jit(solution)/shard_map/ppermute | solution.py:365
  108.6 5.8 %collective-permute-start.17 = (bf16[32,1024]{1,0:T(8,128)(2,1)S(1)}, bf16[32,1024]{1,0:T(8,128)(2,1)S(1)}, u32[]{:S(2)}, u32[]{:S(2)}) collective-permute-start(bf16[32,1024]{1,0:T(8,128)(2,1)S(1)} %get-tuple-element.48), channel_id=1, source_target_pairs={{0,2},{1,3},{2,0},{3,1},{4,6},{5,7},{6,4},{7,5},{8,10},{9,11},{10,... | collective-permute-start | bytes 196616 | tf_op jit(solution)/shard_map/ppermute | solution.py:365
  111.2 5.5 %collective-permute-start.18 = (bf16[32,1024]{1,0:T(8,128)(2,1)S(1)}, bf16[32,1024]{1,0:T(8,128)(2,1)S(1)}, u32[]{:S(2)}, u32[]{:S(2)}) collective-permute-start(bf16[32,1024]{1,0:T(8,128)(2,1)S(1)} %get-tuple-element.49), channel_id=1, source_target_pairs={{0,3},{1,0},{2,1},{3,2},{4,7},{5,4},{6,5},{7,6},{8,11},{9,8},{10,9... | collective-permute-start | bytes 196616 | tf_op jit(solution)/shard_map/ppermute | solution.py:365
  (15 other events, 86.5 us)
